TPU v7x, 1024 devices: a whole 4x8x16 slice. The times are simulated.
1024 devices in a mesh: blk: 32 (over z_hi, x, core), group: 32 (over y, z_lo).
Axes of the slice: x: 4, y: 8, z: 16 (z_hi: 4, z_lo: 4; z = z_hi * 4 + z_lo), core: 2. Of those that a mesh axis runs over, the one named last changes fastest.
Arguments:
- images: bfloat16 [32, 32, 256, 1152], P('blk', 'group'), may hold values from -0.56640625 to 0.56640625
- texts: bfloat16 [32, 32, 256, 1152], P('blk', 'group'), may hold values from -0.56640625 to 0.56640625
Outputs:
- image_grad: float32 [32, 32, 256, 1152], P('blk', 'group')
- text_grad: float32 [32, 32, 256, 1152], P('blk', 'group')
All inputs are finite; a program needn't handle non-finite values.
Results may differ from a plain program's by a relative error of at most 0.0018.
Values may be sent and summed in bfloat16 or wider, within the bound.
No kernel may reach another device: no remote copies, remote signals or barrier semaphores. Data moves between devices by JAX's collectives and lax.ppermute only.
A program may use at most 32 MiB of HBM per device.

v0:
```python
import jax
import jax.numpy as jnp
from jax import lax
from jax.sharding import PartitionSpec as P

HOPS = 2


logit_scale = 10.0
logit_bias = -10.0


def shifted(value, axis, steps):
    count = lax.axis_size(axis)
    pairs = [(source, (source + steps) % count) for source in range(count)]
    return lax.ppermute(value, axis, pairs)


def make_coef(image_tile, text_tile, eye_matrix, section_index):
    logits = (
        logit_scale
        * lax.dot_general(
            image_tile, text_tile, (((1,), (1,)), ((), ())), preferred_element_type=jnp.float32
        )
        + logit_bias
    )
    coef = jax.nn.sigmoid(logits)
    if section_index == 0:
        coef = coef - eye_matrix
    return coef.astype(jnp.bfloat16)


def text_term(coef, image_tile):
    return logit_scale * lax.dot_general(
        coef, image_tile, (((0,), (0,)), ((), ())), preferred_element_type=jnp.float32
    )


def body(images, texts):
    own_images = images.reshape(images.shape[2], images.shape[3])
    visiting = texts.reshape(texts.shape[2], texts.shape[3])
    count = own_images.shape[0]
    eye_matrix = (
        lax.broadcasted_iota(jnp.int32, (count, count), 0)
        == lax.broadcasted_iota(jnp.int32, (count, count), 1)
    ).astype(jnp.float32)
    image_total = jnp.zeros(own_images.shape, jnp.float32)
    coefs = []
    for section_index in range(HOPS + 1):
        if section_index > 0:
            visiting = shifted(visiting, "blk", 1)
        coef = make_coef(own_images, visiting, eye_matrix, section_index)
        image_total = image_total + logit_scale * jnp.dot(
            coef, visiting, preferred_element_type=jnp.float32
        )
        coefs.append(coef)
    accum = text_term(coefs[0], own_images)
    for section_index in range(1, HOPS + 1):
        accum = shifted(accum, "blk", 1) + text_term(coefs[section_index], own_images)
    text_total = shifted(accum, "group", 1)
    return (image_total.reshape(images.shape), text_total.reshape(texts.shape))


def solution(mesh):
    in_specs = (P("blk", "group", None, None), P("blk", "group", None, None))
    out_specs = (P("blk", "group", None, None), P("blk", "group", None, None))
    return jax.shard_map(body, mesh=mesh, in_specs=in_specs, out_specs=out_specs, check_vma=False)
```

profile of v0, /device:TPU:32, one launch (start us, length us, event | category | flops | bytes accessed | tf_op | source)
XLA Modules:
  0.0 216.3 jit_solution(1232466458440143566)
XLA Ops:
  0.6 0.0 copy-start
  0.6 1.1 copy-done
  1.7 1.5 fusion.19
  3.2 0.0 copy-start.1
  3.2 0.4 convolution_multiply_fusion.2
  3.5 1.9 collective-permute-start.2
  5.5 3.5 %collective-permute-start = (bf16[256,1152]{1,0:T(8,128)(2,1)S(1)}, bf16[256,1152]{1,0:T(8,128)(2,1)S(1)}, u32[]{:S(2)}, u32[]{:S(2)}) collective-permute-start(bf16[256,1152]{1,0:T(8,128)(2,1)S(1)} %bitcast.32), channel_id=1, source_target_pairs={{0,32},{32,64},{64,96},{96,128},{128,160},{160,192},{192,224},{224... | collective-permute-start | bytes 1769480 | tf_op jit(solution)/shard_map/ppermute | solution.py:16
  9.0 35.2 %collective-permute-done = bf16[256,1152]{1,0:T(8,128)(2,1)S(1)} collective-permute-done((bf16[256,1152]{1,0:T(8,128)(2,1)S(1)}, bf16[256,1152]{1,0:T(8,128)(2,1)S(1)}, u32[]{:S(2)}, u32[]{:S(2)}) %collective-permute-start) | collective-permute-done | bytes 589856 | tf_op jit(solution)/shard_map/ppermute | solution.py:16
  44.2 0.4 fusion.20
  44.6 0.0 collective-permute-done.2
  44.6 0.4 fusion.1
  45.0 1.9 collective-permute-start.3
  46.9 1.9 collective-permute-start.1
  48.9 143.5 %collective-permute-done.1 = bf16[256,1152]{1,0:T(8,128)(2,1)S(1)} collective-permute-done((bf16[256,1152]{1,0:T(8,128)(2,1)S(1)}, bf16[256,1152]{1,0:T(8,128)(2,1)S(1)}, u32[]{:S(2)}, u32[]{:S(2)}) %collective-permute-start.1) | collective-permute-done | bytes 589856 | tf_op jit(solution)/shard_map/ppermute | solution.py:16
  192.4 0.4 fusion.21
  192.8 0.4 convolution_multiply_fusion
  193.2 0.0 collective-permute-done.3
  193.2 0.1 add.39
  193.3 1.9 collective-permute-start.4
  195.3 0.3 fusion.28
  195.6 0.3 convolution_add_fusion.1
  196.0 1.4 fusion.2
  197.3 18.0 %collective-permute-done.4 = f32[256,1152]{1,0:T(8,128)S(1)} collective-permute-done((f32[256,1152]{1,0:T(8,128)S(1)}, f32[256,1152]{1,0:T(8,128)S(1)}, u32[]{:S(2)}, u32[]{:S(2)}) %collective-permute-start.4) | collective-permute-done | bytes 1179680 | tf_op jit(solution)/shard_map/ppermute | solution.py:16
  215.3 1.0 copy.5
  (1 shorter events, 0.0 us)
Async XLA Ops:
  0.6 1.1 copy-start
  3.2 2.3 %copy-start.1 = (bf16[1,1,256,1152]{3,2,1,0:T(8,128)(2,1)S(1)}, bf16[1,1,256,1152]{3,2,1,0:T(8,128)(2,1)}, u32[]{:S(2)}) copy-start(bf16[1,1,256,1152]{3,2,1,0:T(8,128)(2,1)} %param.3) | copy-start | bytes 1769476
  3.5 41.1 %collective-permute-start.2 = (f32[256,1152]{1,0:T(8,128)S(1)}, f32[256,1152]{1,0:T(8,128)S(1)}, u32[]{:S(2)}, u32[]{:S(2)}) collective-permute-start(f32[256,1152]{1,0:T(8,128)S(1)} %convolution_multiply_fusion.2), channel_id=1, source_target_pairs={{0,32},{32,64},{64,96},{96,128},{128,160},{160,192},{192,224},{224... | collective-permute-start | bytes 3538952 | tf_op jit(solution)/shard_map/ppermute | solution.py:16
  5.5 38.7 %collective-permute-start = (bf16[256,1152]{1,0:T(8,128)(2,1)S(1)}, bf16[256,1152]{1,0:T(8,128)(2,1)S(1)}, u32[]{:S(2)}, u32[]{:S(2)}) collective-permute-start(bf16[256,1152]{1,0:T(8,128)(2,1)S(1)} %bitcast.32), channel_id=1, source_target_pairs={{0,32},{32,64},{64,96},{96,128},{128,160},{160,192},{192,224},{224... | collective-permute-start | bytes 1769480 | tf_op jit(solution)/shard_map/ppermute | solution.py:16
  45.0 148.2 %collective-permute-start.3 = (f32[256,1152]{1,0:T(8,128)S(1)}, f32[256,1152]{1,0:T(8,128)S(1)}, u32[]{:S(2)}, u32[]{:S(2)}) collective-permute-start(f32[256,1152]{1,0:T(8,128)S(1)} %fusion.1), channel_id=1, source_target_pairs={{0,32},{32,64},{64,96},{96,128},{128,160},{160,192},{192,224},{224... | collective-permute-start | bytes 3538952 | tf_op jit(solution)/shard_map/ppermute | solution.py:16
  46.9 145.5 %collective-permute-start.1 = (bf16[256,1152]{1,0:T(8,128)(2,1)S(1)}, bf16[256,1152]{1,0:T(8,128)(2,1)S(1)}, u32[]{:S(2)}, u32[]{:S(2)}) collective-permute-start(bf16[256,1152]{1,0:T(8,128)(2,1)S(1)} %collective-permute-done), channel_id=1, source_target_pairs={{0,32},{32,64},{64,96},{96,128},{128,160},{160,192},{192,224},{224... | collective-permute-start | bytes 1769480 | tf_op jit(solution)/shard_map/ppermute | solution.py:16
  193.3 22.0 %collective-permute-start.4 = (f32[256,1152]{1,0:T(8,128)S(1)}, f32[256,1152]{1,0:T(8,128)S(1)}, u32[]{:S(2)}, u32[]{:S(2)}) collective-permute-start(f32[256,1152]{1,0:T(8,128)S(1)} %add.39), channel_id=1, source_target_pairs={{0,1},{1,2},{2,3},{3,4},{4,5},{5,6},{6,7},{7,8},{8,9},{9,10},{10,1... | collective-permute-start | bytes 3538952 | tf_op jit(solution)/shard_map/ppermute | solution.py:16
where the time goes:
time: 217 us; the launch traced here: 216 us
  waiting for transfers between devices  197 us (91%)
  starting transfers between devices  11.2 us (5%)
  matrix products  5.41 us (2%)
    ppermute x5, waiting for transfers between devices, shifted(): return lax.ppermute(value, axis, pairs)  197 us
    ppermute x5, starting transfers between devices, shifted(): return lax.ppermute(value, axis, pairs)  11.2 us
  transfers between devices with their start and end apart: 5, of which 3 were waited for; matrix products, arithmetic and copies ran while one was open for 1% of the time, Pallas kernels for 0%

commit v1 on v0

v1 whole, which is shorter than its diff:
```python
import jax
import jax.numpy as jnp
from jax import lax
from jax.experimental import pallas as pl
from jax.experimental.pallas import tpu as pltpu
from jax.sharding import PartitionSpec as P

SCALE = 10.0
BIAS = -10.0
TOP = 13.0
EXTRA = 16
AXES = ("blk", "group")
NX, NY, NZ = 4, 8, 16


def place(x, y, z, c):
    x, y, z = x % NX, y % NY, z % NZ
    return ((z // 4) * 8 + x * 2 + c) * 32 + y * 4 + z % 4


def pairs(*moves):
    out = []
    for y in range(NY):
        for z in range(NZ):
            for (x0, c0), (x1, dz, c1) in moves:
                out.append((place(x0, y, z, c0), place(x1, y, z + dz, c1)))
    return out


PLANES = ((0, 2), (1, 0), (2, 1))
NEAR = [((x, c), (x + 1, 0, c)) for x in range(3) for c in range(2)]
STRAIGHT = [((3, c), (0, 4, c)) for c in range(2)]
MOVE_ALL = pairs(*NEAR, *STRAIGHT)
MOVE_NEAR = pairs(*NEAR)
MOVE_OUT = [pairs(*(((3, c), (p[c], 0, c)) for c in range(2))) for p in PLANES]
MOVE_ON = [pairs(*(((p[c], c), (0, 4, c)) for c in range(2))) for p in PLANES]
MOVE_SWAP = pairs(*(((x, c), (x, 0, 1 - c)) for x in range(4) for c in range(2)))


def move(value, table):
    return lax.ppermute(value, AXES, table)


def dot_nt(a, b):
    return lax.dot_general(a, b, (((1,), (1,)), ((), ())), preferred_element_type=jnp.float32)


def dot_tn(a, b):
    return lax.dot_general(a, b, (((0,), (0,)), ((), ())), preferred_element_type=jnp.float32)


def coefs(image, text, diagonal):
    out = jax.nn.sigmoid(SCALE * dot_nt(image, text) + BIAS)
    if diagonal:
        shape = out.shape
        eye = lax.broadcasted_iota(jnp.int32, shape, 0) == lax.broadcasted_iota(jnp.int32, shape, 1)
        out = out - eye.astype(jnp.float32)
    return out.astype(jnp.bfloat16)


def split_kernel(images, texts, i_a, i_b, t_a, t_b, rest, sems):
    half = i_a.shape[0]
    low, high = pl.ds(0, half), pl.ds(half, half)
    copies = [
        pltpu.make_async_copy(images.at[high], i_b, sems.at[0]),
        pltpu.make_async_copy(texts.at[low], t_a, sems.at[1]),
        pltpu.make_async_copy(texts.at[high], t_b, sems.at[2]),
        pltpu.make_async_copy(images.at[low], i_a, sems.at[3]),
        pltpu.make_async_copy(images.at[high], rest.at[pl.ds(0, half)], sems.at[4]),
        pltpu.make_async_copy(texts, rest.at[pl.ds(half, 2 * half)], sems.at[5]),
    ]
    for copy in copies:
        copy.start()
    for copy in copies:
        copy.wait()


def pick_kernel(where, head, rest, far0, far1, far2, i0, t0, i2, t2, swap):
    half = head.shape[0]
    i2[:half] = head[...]

    @pl.when(where[0] == 1)
    def _():
        i2[half:] = far0[...]
        t2[:half] = far1[...]
        t2[half:] = far2[...]

    @pl.when(where[0] == 0)
    def _():
        i2[half:] = rest[:half]
        t2[...] = rest[half:]

    @pl.when(where[1] == 1)
    def _():
        swap[: 2 * half] = i2[...]
        swap[2 * half :] = t2[...]

    @pl.when(where[1] == 0)
    def _():
        swap[: 2 * half] = i0[...]
        swap[2 * half :] = t0[...]


def two_kernel(i2, i0, t2, out):
    text = t2[...]
    out[...] = dot_tn(coefs(i2[...], text, True), i2[...]) + dot_tn(coefs(i0[...], text, False), i0[...])


def text_kernel(part, one, t2, code):
    rows = part.shape[0]
    acc = part[...] + dot_tn(coefs(one[:rows], t2[...], False), one[:rows])
    top = jnp.maximum(jnp.max(jnp.abs(acc), axis=(0, 1), keepdims=True), 1e-35)
    power = jnp.ceil(jnp.log2(top))
    z = acc * jnp.exp2(TOP - power)
    z2 = z * z
    z4 = z2 * z2
    code[:rows] = (z4 * z4 * z).astype(jnp.bfloat16)
    code[rows:] = jnp.broadcast_to(power, (code.shape[0] - rows, part.shape[1])).astype(jnp.bfloat16)


def read_kernel(code, out):
    step = out.shape[0]
    rows = code.shape[0] - EXTRA
    start = pl.multiple_of(pl.program_id(0) * step, step)
    y = code[pl.ds(start, step)].astype(jnp.float32)
    power = code[rows : rows + EXTRA].astype(jnp.float32)[:1, :1]
    z = jnp.exp2(jnp.log2(jnp.maximum(jnp.abs(y), 1e-38)) * (1.0 / 9.0)) * (SCALE * jnp.exp2(power - TOP))
    z = jnp.where(jnp.abs(y) < 2e-38, 0.0, z)
    out[...] = jnp.where(y < 0, -z, z)


def image_kernel(i0, t0, one, t2, out):
    rows = i0.shape[0]
    image = i0[...]
    acc = None
    for k, ref in enumerate((t0, one.at[rows:], t2)):
        text = ref[...]
        term = jnp.dot(coefs(image, text, k == 0), text, preferred_element_type=jnp.float32)
        acc = term if acc is None else acc + term
    out[...] = SCALE * acc


def body(images, texts):
    rows, width = images.shape[2:]
    half = rows // 2
    own_i = images.reshape(rows, width)
    own_t = texts.reshape(rows, width)
    blk = lax.axis_index("blk")
    core = blk % 2
    first = (blk // 2) % 4 == 0
    where = jnp.stack([first.astype(jnp.int32), core.astype(jnp.int32)])

    vm = pl.BlockSpec(memory_space=pltpu.VMEM)
    sm = pl.BlockSpec(memory_space=pltpu.SMEM)
    hbm = pl.BlockSpec(memory_space=pltpu.HBM)

    def call(kernel, outs, specs, terms, out_specs=vm, grid=(), scratch=()):
        return pl.pallas_call(
            kernel,
            out_shape=outs,
            in_specs=specs,
            out_specs=out_specs if not isinstance(outs, tuple) else (out_specs,) * len(outs),
            grid=grid,
            scratch_shapes=scratch,
            cost_estimate=pl.CostEstimate(
                flops=terms * 4 * rows * rows * width, bytes_accessed=2 << 20, transcendentals=0
            ),
            compiler_params=pltpu.CompilerParams(vmem_limit_bytes=32 << 20),
        )

    def bf(n):
        return jax.ShapeDtypeStruct((n, width), jnp.bfloat16)

    full = jax.ShapeDtypeStruct((rows, width), jnp.float32)

    i_a, i_b, t_a, t_b, near = call(
        split_kernel,
        (bf(half),) * 4 + (bf(3 * half),),
        [hbm] * 2,
        0,
        scratch=[pltpu.SemaphoreType.DMA((6,))],
    )(own_i, own_t)
    out = [move(p, t) for p, t in zip((i_b, t_a, t_b), MOVE_OUT)]
    head = move(i_a, MOVE_ALL)
    rest = move(near, MOVE_NEAR)
    far = [move(p, t) for p, t in zip(out, MOVE_ON)]
    i2, t2, swap = call(pick_kernel, (bf(rows), bf(rows), bf(2 * rows)), [sm] + [vm] * 7, 0)(
        where, head, rest, *far, own_i, own_t
    )
    one = move(swap, MOVE_SWAP)
    part = call(two_kernel, full, [vm] * 3, 2)(i2, own_i, t2)
    code = call(text_kernel, bf(rows + EXTRA), [vm] * 3, 1)(part, one, t2)
    count = lax.axis_size("group")
    got = lax.ppermute(code, "group", [(s, (s + 1) % count) for s in range(count)])
    image_grad = call(image_kernel, full, [vm] * 4, 3)(own_i, own_t, one, t2)
    cut = rows // 4
    text_grad = call(
        read_kernel, full, [vm], 0, out_specs=pl.BlockSpec((cut, width), lambda n: (n, 0)), grid=(rows // cut,)
    )(got)
    return image_grad.reshape(images.shape), text_grad.reshape(texts.shape)


def solution(mesh):
    spec = P("blk", "group", None, None)
    return jax.shard_map(body, mesh=mesh, in_specs=(spec, spec), out_specs=(spec, spec), check_vma=False)
```

time: 217 us -> 100 us (0.46)
  the two profiles are of different devices: /device:TPU:32 before, /device:TPU:1 now
where the time goes in v1:
time: 100 us; the launch traced here: 99.7 us
  starting transfers between devices  47 us (47%)
  waiting for transfers between devices  40.1 us (40%)
  Pallas kernels  9.61 us (10%)
  local copies, waits for them, and re-layouts  2.13 us (2%)
    ppermute x9, starting transfers between devices, move(): return lax.ppermute(value, AXES, table)  36 us
    ppermute x1, waiting for transfers between devices, body(): lax.ppermute(code, 'group', [(s, (s + 1) % count) for s in range(count)])  20.3 us
    ppermute x9, waiting for transfers between devices, move(): return lax.ppermute(value, AXES, table)  19.7 us
    ppermute x1, starting transfers between devices, body(): lax.ppermute(code, 'group', [(s, (s + 1) % count) for s in range(count)])  11 us
    pallas_call x1, Pallas kernels, body(): image_grad = call(image_kernel, full, [vm] * 4, 3)(own_i, own_t, one, t2)  2.76 us
    unnamed x8, local copies, waits for them, and re-layouts  2.13 us
    pallas_call x1, Pallas kernels, body(): call(read_kernel, full, [vm], 0, out_specs=pl.BlockSpec((cut, width), lam...  2.03 us
  transfers between devices with their start and end apart: 10, of which 6 were waited for; matrix products, arithmetic and copies ran while one was open for 0% of the time, Pallas kernels for 4%

profile of v1, /device:TPU:1, one launch (start us, length us, event | category | flops | bytes accessed | tf_op | source)
XLA Modules:
  0.0 99.7 jit_solution(9010598278632640960)
XLA Ops:
  0.6 1.1 %copy-done = bf16[1,1,256,1152]{3,2,1,0:T(8,128)(2,1)S(1)} copy-done((bf16[1,1,256,1152]{3,2,1,0:T(8,128)(2,1)S(1)}, bf16[1,1,256,1152]{3,2,1,0:T(8,128)(2,1)}, u32[]{:S(2)}) %copy-start) | copy-done | bytes 589848
  1.7 1.1 %copy-done.2 = bf16[1,1,256,1152]{3,2,1,0:T(8,128)(2,1)S(1)} copy-done((bf16[1,1,256,1152]{3,2,1,0:T(8,128)(2,1)S(1)}, bf16[1,1,256,1152]{3,2,1,0:T(8,128)(2,1)}, u32[]{:S(2)}) %copy-start.2) | copy-done | bytes 589848
  2.8 1.4 %shard_map.41 = (bf16[128,1152]{1,0:T(8,128)(2,1)S(1)}, bf16[128,1152]{1,0:T(8,128)(2,1)S(1)}, bf16[128,1152]{1,0:T(8,128)(2,1)S(1)}, bf16[128,1152]{1,0:T(8,128)(2,1)S(1)}, bf16[384,1152]{1,0:T(8,128)(2,1)}) custom-call(bf16[256,1152]{1,0:T(8,128)(2,1)S(1)} %bitcast.6, bf16[256,1152]{1,0:T(8,128)(2,1)S(1)} %bitcast.10), custom_call_target="tpu_custom_call" | custom-call | bytes 2097152 | tf_op jit(solution)/shard_map/pallas_call | solution.py:176
  4.2 4.0 %collective-permute-start.1 = (bf16[384,1152]{1,0:T(8,128)(2,1)}, bf16[384,1152]{1,0:T(8,128)(2,1)S(1)}, u32[]{:S(2)}, u32[]{:S(2)}) collective-permute-start(bf16[384,1152]{1,0:T(8,128)(2,1)} %get-tuple-element.11), channel_id=1, source_target_pairs={{0,64},{32,96},{64,128},{96,160},{128,192},{160,224},{1,65},{33,97... | collective-permute-start | bytes 2654216 | tf_op jit(solution)/shard_map/ppermute | solution.py:41
  8.2 1.4 %collective-permute-start.2 = (bf16[128,1152]{1,0:T(8,128)(2,1)S(1)}, bf16[128,1152]{1,0:T(8,128)(2,1)}, u32[]{:S(2)}, u32[]{:S(2)}) collective-permute-start(bf16[128,1152]{1,0:T(8,128)(2,1)S(1)} %get-tuple-element.12), channel_id=1, source_target_pairs={{192,0},{224,160},{193,1},{225,161},{194,2},{226,162},{195,3},{227... | collective-permute-start | bytes 884744 | tf_op jit(solution)/shard_map/ppermute | solution.py:41
  9.5 1.3 %collective-permute-start.4 = (bf16[128,1152]{1,0:T(8,128)(2,1)S(1)}, bf16[128,1152]{1,0:T(8,128)(2,1)}, u32[]{:S(2)}, u32[]{:S(2)}) collective-permute-start(bf16[128,1152]{1,0:T(8,128)(2,1)S(1)} %get-tuple-element.13), channel_id=1, source_target_pairs={{192,64},{224,32},{193,65},{225,33},{194,66},{226,34},{195,67},{22... | collective-permute-start | bytes 884744 | tf_op jit(solution)/shard_map/ppermute | solution.py:41
  10.8 1.4 %collective-permute-start.6 = (bf16[128,1152]{1,0:T(8,128)(2,1)S(1)}, bf16[128,1152]{1,0:T(8,128)(2,1)}, u32[]{:S(2)}, u32[]{:S(2)}) collective-permute-start(bf16[128,1152]{1,0:T(8,128)(2,1)S(1)} %get-tuple-element.14), channel_id=1, source_target_pairs={{192,128},{224,96},{193,129},{225,97},{194,130},{226,98},{195,131}... | collective-permute-start | bytes 884744 | tf_op jit(solution)/shard_map/ppermute | solution.py:41
  12.2 3.0 %collective-permute-start = (bf16[128,1152]{1,0:T(8,128)(2,1)S(1)}, bf16[128,1152]{1,0:T(8,128)(2,1)S(1)}, u32[]{:S(2)}, u32[]{:S(2)}) collective-permute-start(bf16[128,1152]{1,0:T(8,128)(2,1)S(1)} %get-tuple-element.10), channel_id=1, source_target_pairs={{0,64},{32,96},{64,128},{96,160},{128,192},{160,224},{192,256},{22... | collective-permute-start | bytes 884744 | tf_op jit(solution)/shard_map/ppermute | solution.py:41
  15.3 1.3 %collective-permute-start.3 = (bf16[128,1152]{1,0:T(8,128)(2,1)}, bf16[128,1152]{1,0:T(8,128)(2,1)S(1)}, u32[]{:S(2)}, u32[]{:S(2)}) collective-permute-start(bf16[128,1152]{1,0:T(8,128)(2,1)} %collective-permute-done.2), channel_id=1, source_target_pairs={{0,256},{160,288},{1,257},{161,289},{2,258},{162,290},{3,259},{163... | collective-permute-start | bytes 884744 | tf_op jit(solution)/shard_map/ppermute | solution.py:41
  16.6 2.4 %collective-permute-done.4 = bf16[128,1152]{1,0:T(8,128)(2,1)} collective-permute-done((bf16[128,1152]{1,0:T(8,128)(2,1)S(1)}, bf16[128,1152]{1,0:T(8,128)(2,1)}, u32[]{:S(2)}, u32[]{:S(2)}) %collective-permute-start.4) | collective-permute-done | bytes 294944 | tf_op jit(solution)/shard_map/ppermute | solution.py:41
  18.9 13.2 %collective-permute-start.5 = (bf16[128,1152]{1,0:T(8,128)(2,1)}, bf16[128,1152]{1,0:T(8,128)(2,1)S(1)}, u32[]{:S(2)}, u32[]{:S(2)}) collective-permute-start(bf16[128,1152]{1,0:T(8,128)(2,1)} %collective-permute-done.4), channel_id=1, source_target_pairs={{64,256},{32,288},{65,257},{33,289},{66,258},{34,290},{67,259},{35... | collective-permute-start | bytes 884744 | tf_op jit(solution)/shard_map/ppermute | solution.py:41
  32.2 1.3 %collective-permute-start.7 = (bf16[128,1152]{1,0:T(8,128)(2,1)}, bf16[128,1152]{1,0:T(8,128)(2,1)S(1)}, u32[]{:S(2)}, u32[]{:S(2)}) collective-permute-start(bf16[128,1152]{1,0:T(8,128)(2,1)} %collective-permute-done.6), channel_id=1, source_target_pairs={{128,256},{96,288},{129,257},{97,289},{130,258},{98,290},{131,259}... | collective-permute-start | bytes 884744 | tf_op jit(solution)/shard_map/ppermute | solution.py:41
  33.6 10.5 %collective-permute-done.head = bf16[128,1152]{1,0:T(8,128)(2,1)S(1)} collective-permute-done((bf16[128,1152]{1,0:T(8,128)(2,1)S(1)}, bf16[128,1152]{1,0:T(8,128)(2,1)S(1)}, u32[]{:S(2)}, u32[]{:S(2)}) %collective-permute-start) | collective-permute-done | bytes 294944 | tf_op jit(solution)/shard_map/ppermute | solution.py:41
  44.1 3.3 %collective-permute-done.5.far1 = bf16[128,1152]{1,0:T(8,128)(2,1)S(1)} collective-permute-done((bf16[128,1152]{1,0:T(8,128)(2,1)}, bf16[128,1152]{1,0:T(8,128)(2,1)S(1)}, u32[]{:S(2)}, u32[]{:S(2)}) %collective-permute-start.5) | collective-permute-done | bytes 294944 | tf_op jit(solution)/shard_map/ppermute | solution.py:41
  47.4 2.2 %collective-permute-done.7.far2 = bf16[128,1152]{1,0:T(8,128)(2,1)S(1)} collective-permute-done((bf16[128,1152]{1,0:T(8,128)(2,1)}, bf16[128,1152]{1,0:T(8,128)(2,1)S(1)}, u32[]{:S(2)}, u32[]{:S(2)}) %collective-permute-start.7) | collective-permute-done | bytes 294944 | tf_op jit(solution)/shard_map/ppermute | solution.py:41
  49.6 0.7 shard_map.42
  50.3 9.2 %collective-permute-start.8 = (bf16[512,1152]{1,0:T(8,128)(2,1)S(1)}, bf16[512,1152]{1,0:T(8,128)(2,1)S(1)}, u32[]{:S(2)}, u32[]{:S(2)}) collective-permute-start(bf16[512,1152]{1,0:T(8,128)(2,1)S(1)} %get-tuple-element.15), channel_id=1, source_target_pairs={{0,32},{32,0},{64,96},{96,64},{128,160},{160,128},{192,224},{224,1... | collective-permute-start | bytes 3538952 | tf_op jit(solution)/shard_map/ppermute | solution.py:41
  59.5 1.1 %shard_map.44.part = f32[256,1152]{1,0:T(8,128)S(1)} custom-call(bf16[256,1152]{1,0:T(8,128)(2,1)S(1)} %get-tuple-element.17.i2, bf16[256,1152]{1,0:T(8,128)(2,1)S(1)} %bitcast.8, bf16[256,1152]{1,0:T(8,128)(2,1)S(1)} %get-tuple-element.16.t2), custom_call_target="tpu_custom_call" | custom-call | flops 603979776 | bytes 2097152 | tf_op jit(solution)/shard_map/pallas_call | solution.py:191
  60.6 1.4 %collective-permute-done.8.one = bf16[512,1152]{1,0:T(8,128)(2,1)S(1)} collective-permute-done((bf16[512,1152]{1,0:T(8,128)(2,1)S(1)}, bf16[512,1152]{1,0:T(8,128)(2,1)S(1)}, u32[]{:S(2)}, u32[]{:S(2)}) %collective-permute-start.8) | collective-permute-done | bytes 1179680 | tf_op jit(solution)/shard_map/ppermute | solution.py:41
  61.9 1.6 %shard_map.45 = bf16[272,1152]{1,0:T(8,128)(2,1)S(1)} custom-call(f32[256,1152]{1,0:T(8,128)S(1)} %shard_map.44.part, bf16[512,1152]{1,0:T(8,128)(2,1)S(1)} %collective-permute-done.8.one, bf16[256,1152]{1,0:T(8,128)(2,1)S(1)} %get-tuple-element.16.t2), custom_call_target="tpu_custom_call" | custom-call | flops 301989888 | bytes 2097152 | tf_op jit(solution)/shard_map/pallas_call | solution.py:192
  63.6 11.0 %collective-permute-start.9 = (bf16[272,1152]{1,0:T(8,128)(2,1)S(1)}, bf16[272,1152]{1,0:T(8,128)(2,1)S(1)}, u32[]{:S(2)}, u32[]{:S(2)}) collective-permute-start(bf16[272,1152]{1,0:T(8,128)(2,1)S(1)} %shard_map.45), channel_id=1, source_target_pairs={{0,1},{1,2},{2,3},{3,4},{4,5},{5,6},{6,7},{7,8},{8,9},{9,10},{10,1... | collective-permute-start | bytes 1880072 | tf_op jit(solution)/shard_map/ppermute | solution.py:194
  74.6 2.8 %shard_map.43 = f32[256,1152]{1,0:T(8,128)} custom-call(bf16[256,1152]{1,0:T(8,128)(2,1)S(1)} %bitcast.9, bf16[256,1152]{1,0:T(8,128)(2,1)S(1)} %bitcast.12, bf16[512,1152]{1,0:T(8,128)(2,1)S(1)} %collective-permute-done.8.one, bf16[256,1152]{1,0:T(8,128)(2,1)S(1)} %get-tuple-element.16.t2), custom_call_target="tpu_custom_call" | custom-call | flops 905969664 | bytes 2097152 | tf_op jit(solution)/shard_map/pallas_call | solution.py:195
  77.3 20.3 %collective-permute-done.9.code = bf16[272,1152]{1,0:T(8,128)(2,1)S(1)} collective-permute-done((bf16[272,1152]{1,0:T(8,128)(2,1)S(1)}, bf16[272,1152]{1,0:T(8,128)(2,1)S(1)}, u32[]{:S(2)}, u32[]{:S(2)}) %collective-permute-start.9) | collective-permute-done | bytes 626720 | tf_op jit(solution)/shard_map/ppermute | solution.py:194
  97.6 2.0 %shard_map.46 = f32[256,1152]{1,0:T(8,128)} custom-call(bf16[272,1152]{1,0:T(8,128)(2,1)S(1)} %collective-permute-done.9.code), custom_call_target="tpu_custom_call" | custom-call | bytes 2097152 | tf_op jit(solution)/shard_map/pallas_call | solution.py:197
  (11 shorter events, 0.1 us)
Async XLA Ops:
  0.6 1.1 %copy-start = (bf16[1,1,256,1152]{3,2,1,0:T(8,128)(2,1)S(1)}, bf16[1,1,256,1152]{3,2,1,0:T(8,128)(2,1)}, u32[]{:S(2)}) copy-start(bf16[1,1,256,1152]{3,2,1,0:T(8,128)(2,1)} %param.2) | copy-start | bytes 1769476
  1.7 1.1 %copy-start.2 = (bf16[1,1,256,1152]{3,2,1,0:T(8,128)(2,1)S(1)}, bf16[1,1,256,1152]{3,2,1,0:T(8,128)(2,1)}, u32[]{:S(2)}) copy-start(bf16[1,1,256,1152]{3,2,1,0:T(8,128)(2,1)} %param.3) | copy-start | bytes 1769476
  2.8 46.8 %copy-start.1 = (bf16[1,1,256,1152]{3,2,1,0:T(8,128)(2,1)S(1)}, bf16[1,1,256,1152]{3,2,1,0:T(8,128)(2,1)}, u32[]{:S(2)}) copy-start(bf16[1,1,256,1152]{3,2,1,0:T(8,128)(2,1)} %param.2) | copy-start | bytes 1769476
  2.8 46.8 %copy-start.3 = (bf16[1,1,256,1152]{3,2,1,0:T(8,128)(2,1)S(1)}, bf16[1,1,256,1152]{3,2,1,0:T(8,128)(2,1)}, u32[]{:S(2)}) copy-start(bf16[1,1,256,1152]{3,2,1,0:T(8,128)(2,1)} %param.3) | copy-start | bytes 1769476
  4.2 45.4 %collective-permute-start.1 = (bf16[384,1152]{1,0:T(8,128)(2,1)}, bf16[384,1152]{1,0:T(8,128)(2,1)S(1)}, u32[]{:S(2)}, u32[]{:S(2)}) collective-permute-start(bf16[384,1152]{1,0:T(8,128)(2,1)} %get-tuple-element.11), channel_id=1, source_target_pairs={{0,64},{32,96},{64,128},{96,160},{128,192},{160,224},{1,65},{33,97... | collective-permute-start | bytes 2654216 | tf_op jit(solution)/shard_map/ppermute | solution.py:41
  8.2 7.1 %collective-permute-start.2 = (bf16[128,1152]{1,0:T(8,128)(2,1)S(1)}, bf16[128,1152]{1,0:T(8,128)(2,1)}, u32[]{:S(2)}, u32[]{:S(2)}) collective-permute-start(bf16[128,1152]{1,0:T(8,128)(2,1)S(1)} %get-tuple-element.12), channel_id=1, source_target_pairs={{192,0},{224,160},{193,1},{225,161},{194,2},{226,162},{195,3},{227... | collective-permute-start | bytes 884744 | tf_op jit(solution)/shard_map/ppermute | solution.py:41
  9.5 9.4 %collective-permute-start.4 = (bf16[128,1152]{1,0:T(8,128)(2,1)S(1)}, bf16[128,1152]{1,0:T(8,128)(2,1)}, u32[]{:S(2)}, u32[]{:S(2)}) collective-permute-start(bf16[128,1152]{1,0:T(8,128)(2,1)S(1)} %get-tuple-element.13), channel_id=1, source_target_pairs={{192,64},{224,32},{193,65},{225,33},{194,66},{226,34},{195,67},{22... | collective-permute-start | bytes 884744 | tf_op jit(solution)/shard_map/ppermute | solution.py:41
  10.8 21.3 %collective-permute-start.6 = (bf16[128,1152]{1,0:T(8,128)(2,1)S(1)}, bf16[128,1152]{1,0:T(8,128)(2,1)}, u32[]{:S(2)}, u32[]{:S(2)}) collective-permute-start(bf16[128,1152]{1,0:T(8,128)(2,1)S(1)} %get-tuple-element.14), channel_id=1, source_target_pairs={{192,128},{224,96},{193,129},{225,97},{194,130},{226,98},{195,131}... | collective-permute-start | bytes 884744 | tf_op jit(solution)/shard_map/ppermute | solution.py:41
  12.2 31.9 %collective-permute-start = (bf16[128,1152]{1,0:T(8,128)(2,1)S(1)}, bf16[128,1152]{1,0:T(8,128)(2,1)S(1)}, u32[]{:S(2)}, u32[]{:S(2)}) collective-permute-start(bf16[128,1152]{1,0:T(8,128)(2,1)S(1)} %get-tuple-element.10), channel_id=1, source_target_pairs={{0,64},{32,96},{64,128},{96,160},{128,192},{160,224},{192,256},{22... | collective-permute-start | bytes 884744 | tf_op jit(solution)/shard_map/ppermute | solution.py:41
  15.3 28.8 %collective-permute-start.3 = (bf16[128,1152]{1,0:T(8,128)(2,1)}, bf16[128,1152]{1,0:T(8,128)(2,1)S(1)}, u32[]{:S(2)}, u32[]{:S(2)}) collective-permute-start(bf16[128,1152]{1,0:T(8,128)(2,1)} %collective-permute-done.2), channel_id=1, source_target_pairs={{0,256},{160,288},{1,257},{161,289},{2,258},{162,290},{3,259},{163... | collective-permute-start | bytes 884744 | tf_op jit(solution)/shard_map/ppermute | solution.py:41
  18.9 28.4 %collective-permute-start.5 = (bf16[128,1152]{1,0:T(8,128)(2,1)}, bf16[128,1152]{1,0:T(8,128)(2,1)S(1)}, u32[]{:S(2)}, u32[]{:S(2)}) collective-permute-start(bf16[128,1152]{1,0:T(8,128)(2,1)} %collective-permute-done.4), channel_id=1, source_target_pairs={{64,256},{32,288},{65,257},{33,289},{66,258},{34,290},{67,259},{35... | collective-permute-start | bytes 884744 | tf_op jit(solution)/shard_map/ppermute | solution.py:41
  32.2 17.4 %collective-permute-start.7 = (bf16[128,1152]{1,0:T(8,128)(2,1)}, bf16[128,1152]{1,0:T(8,128)(2,1)S(1)}, u32[]{:S(2)}, u32[]{:S(2)}) collective-permute-start(bf16[128,1152]{1,0:T(8,128)(2,1)} %collective-permute-done.6), channel_id=1, source_target_pairs={{128,256},{96,288},{129,257},{97,289},{130,258},{98,290},{131,259}... | collective-permute-start | bytes 884744 | tf_op jit(solution)/shard_map/ppermute | solution.py:41
  50.3 11.6 %collective-permute-start.8 = (bf16[512,1152]{1,0:T(8,128)(2,1)S(1)}, bf16[512,1152]{1,0:T(8,128)(2,1)S(1)}, u32[]{:S(2)}, u32[]{:S(2)}) collective-permute-start(bf16[512,1152]{1,0:T(8,128)(2,1)S(1)} %get-tuple-element.15), channel_id=1, source_target_pairs={{0,32},{32,0},{64,96},{96,64},{128,160},{160,128},{192,224},{224,1... | collective-permute-start | bytes 3538952 | tf_op jit(solution)/shard_map/ppermute | solution.py:41
  63.6 34.1 %collective-permute-start.9 = (bf16[272,1152]{1,0:T(8,128)(2,1)S(1)}, bf16[272,1152]{1,0:T(8,128)(2,1)S(1)}, u32[]{:S(2)}, u32[]{:S(2)}) collective-permute-start(bf16[272,1152]{1,0:T(8,128)(2,1)S(1)} %shard_map.45), channel_id=1, source_target_pairs={{0,1},{1,2},{2,3},{3,4},{4,5},{5,6},{6,7},{7,8},{8,9},{9,10},{10,1... | collective-permute-start | bytes 1880072 | tf_op jit(solution)/shard_map/ppermute | solution.py:194

commit v2 on v1

--- a/solution.py
+++ b/solution.py
@@ -58,16 +58,12 @@
     return out.astype(jnp.bfloat16)
 
 
-def split_kernel(images, texts, i_a, i_b, t_a, t_b, rest, sems):
-    half = i_a.shape[0]
-    low, high = pl.ds(0, half), pl.ds(half, half)
+def near_kernel(images, texts, after0, after1, after2, rest, sems):
+    half = after0.shape[0]
+    high = pl.ds(half, half)
     copies = [
-        pltpu.make_async_copy(images.at[high], i_b, sems.at[0]),
-        pltpu.make_async_copy(texts.at[low], t_a, sems.at[1]),
-        pltpu.make_async_copy(texts.at[high], t_b, sems.at[2]),
-        pltpu.make_async_copy(images.at[low], i_a, sems.at[3]),
-        pltpu.make_async_copy(images.at[high], rest.at[pl.ds(0, half)], sems.at[4]),
-        pltpu.make_async_copy(texts, rest.at[pl.ds(half, 2 * half)], sems.at[5]),
+        pltpu.make_async_copy(images.at[high], rest.at[pl.ds(0, half)], sems.at[0]),
+        pltpu.make_async_copy(texts, rest.at[pl.ds(half, 2 * half)], sems.at[1]),
     ]
     for copy in copies:
         copy.start()
@@ -75,47 +71,63 @@
         copy.wait()
 
 
-def pick_kernel(where, head, rest, far0, far1, far2, i0, t0, i2, t2, swap):
+def pick_images(where, head, rest, far0, i0, i2, swap):
     half = head.shape[0]
     i2[:half] = head[...]
 
     @pl.when(where[0] == 1)
     def _():
         i2[half:] = far0[...]
+
+    @pl.when(where[0] == 0)
+    def _():
+        i2[half:] = rest[:half]
+
+    @pl.when(where[1] == 1)
+    def _():
+        swap[...] = i2[...]
+
+    @pl.when(where[1] == 0)
+    def _():
+        swap[...] = i0[...]
+
+
+def part_kernel(where, rest, far1, far2, i2, i0, t2, out):
+    half = far1.shape[0]
+
+    @pl.when(where[0] == 1)
+    def _():
         t2[:half] = far1[...]
         t2[half:] = far2[...]
 
     @pl.when(where[0] == 0)
     def _():
-        i2[half:] = rest[:half]
         t2[...] = rest[half:]
 
-    @pl.when(where[1] == 1)
-    def _():
-        swap[: 2 * half] = i2[...]
-        swap[2 * half :] = t2[...]
-
-    @pl.when(where[1] == 0)
-    def _():
-        swap[: 2 * half] = i0[...]
-        swap[2 * half :] = t0[...]
-
-
-def two_kernel(i2, i0, t2, out):
     text = t2[...]
     out[...] = dot_tn(coefs(i2[...], text, True), i2[...]) + dot_tn(coefs(i0[...], text, False), i0[...])
 
 
-def text_kernel(part, one, t2, code):
+def text_kernel(part, i1, t2, code):
     rows = part.shape[0]
-    acc = part[...] + dot_tn(coefs(one[:rows], t2[...], False), one[:rows])
+    acc = part[...] + dot_tn(coefs(i1[...], t2[...], False), i1[...])
     top = jnp.maximum(jnp.max(jnp.abs(acc), axis=(0, 1), keepdims=True), 1e-35)
     power = jnp.ceil(jnp.log2(top))
     z = acc * jnp.exp2(TOP - power)
     z2 = z * z
     z4 = z2 * z2
     code[:rows] = (z4 * z4 * z).astype(jnp.bfloat16)
-    code[rows:] = jnp.broadcast_to(power, (code.shape[0] - rows, part.shape[1])).astype(jnp.bfloat16)
+    code[rows:] = jnp.broadcast_to(power, (code.shape[0] - rows, acc.shape[1])).astype(jnp.bfloat16)
+
+
+def pick_texts(where, code, t2, t0, swap):
+    @pl.when(where[1] == 1)
+    def _():
+        swap[...] = t2[...]
+
+    @pl.when(where[1] == 0)
+    def _():
+        swap[...] = t0[...]
 
 
 def read_kernel(code, out):
@@ -129,11 +141,10 @@
     out[...] = jnp.where(y < 0, -z, z)
 
 
-def image_kernel(i0, t0, one, t2, out):
-    rows = i0.shape[0]
+def image_kernel(i0, t0, t1, t2, out):
     image = i0[...]
     acc = None
-    for k, ref in enumerate((t0, one.at[rows:], t2)):
+    for k, ref in enumerate((t0, t1, t2)):
         text = ref[...]
         term = jnp.dot(coefs(image, text, k == 0), text, preferred_element_type=jnp.float32)
         acc = term if acc is None else acc + term
@@ -152,7 +163,7 @@
 
     vm = pl.BlockSpec(memory_space=pltpu.VMEM)
     sm = pl.BlockSpec(memory_space=pltpu.SMEM)
-    hbm = pl.BlockSpec(memory_space=pltpu.HBM)
+    anywhere = pl.BlockSpec(memory_space=pl.ANY)
 
     def call(kernel, outs, specs, terms, out_specs=vm, grid=(), scratch=()):
         return pl.pallas_call(
@@ -173,26 +184,21 @@
 
     full = jax.ShapeDtypeStruct((rows, width), jnp.float32)
 
-    i_a, i_b, t_a, t_b, near = call(
-        split_kernel,
-        (bf(half),) * 4 + (bf(3 * half),),
-        [hbm] * 2,
-        0,
-        scratch=[pltpu.SemaphoreType.DMA((6,))],
-    )(own_i, own_t)
-    out = [move(p, t) for p, t in zip((i_b, t_a, t_b), MOVE_OUT)]
-    head = move(i_a, MOVE_ALL)
+    out = [move(p, t) for p, t in zip((own_i[half:], own_t[:half], own_t[half:]), MOVE_OUT)]
+    head = move(own_i[:half], MOVE_ALL)
+    near = call(
+        near_kernel, bf(3 * half), [anywhere] * 5, 0, scratch=[pltpu.SemaphoreType.DMA((2,))]
+    )(own_i, own_t, *out)
     rest = move(near, MOVE_NEAR)
     far = [move(p, t) for p, t in zip(out, MOVE_ON)]
-    i2, t2, swap = call(pick_kernel, (bf(rows), bf(rows), bf(2 * rows)), [sm] + [vm] * 7, 0)(
-        where, head, rest, *far, own_i, own_t
-    )
-    one = move(swap, MOVE_SWAP)
-    part = call(two_kernel, full, [vm] * 3, 2)(i2, own_i, t2)
-    code = call(text_kernel, bf(rows + EXTRA), [vm] * 3, 1)(part, one, t2)
+    i2, swap_i = call(pick_images, (bf(rows),) * 2, [sm] + [vm] * 4, 0)(where, head, rest, far[0], own_i)
+    i1 = move(swap_i, MOVE_SWAP)
+    t2, part = call(part_kernel, (bf(rows), full), [sm] + [vm] * 5, 60)(where, rest, far[1], far[2], i2, own_i)
+    code = call(text_kernel, bf(rows + EXTRA), [vm] * 3, 1)(part, i1, t2)
     count = lax.axis_size("group")
     got = lax.ppermute(code, "group", [(s, (s + 1) % count) for s in range(count)])
-    image_grad = call(image_kernel, full, [vm] * 4, 3)(own_i, own_t, one, t2)
+    t1 = move(call(pick_texts, bf(rows), [sm, anywhere] + [vm] * 2, 0)(where, code, t2, own_t), MOVE_SWAP)
+    image_grad = call(image_kernel, full, [vm] * 4, 0)(own_i, own_t, t1, t2)
     cut = rows // 4
     text_grad = call(
         read_kernel, full, [vm], 0, out_specs=pl.BlockSpec((cut, width), lambda n: (n, 0)), grid=(rows // cut,)

time: 100 us -> 103 us (1.030)
  waiting for transfers between devices: 40.1 us -> 42.8 us
    ppermute x1, waiting for transfers between devices: 20.3 us -> 23.1 us  [body(): lax.ppermute(code, 'group', [(s, (s + 1) % count) for s in range(count)])]
    unnamed x8 -> x4, local copies, waits for them, and re-layouts: 2.13 us -> 0.01 us
    slice x0 -> x2, local copies, waits for them, and re-layouts: none -> 1.95 us  [the longest x1 1.9 us: body(): head = move(own_i[:half], MOVE_ALL)]
    ppermute x1, starting transfers between devices: 11 us -> 9.31 us  [body(): lax.ppermute(code, 'group', [(s, (s + 1) % count) for s in range(count)])]
    ppermute x9 -> x10, starting transfers between devices: 36 us -> 37.4 us  [move(): return lax.ppermute(value, AXES, table)]
    pallas_call x5 -> x6, Pallas kernels: 7.57 us -> 8.56 us  [the longest x1 2.76 us: body(): image_grad = call(image_kernel, full, [vm] * 4, 0)(own_i, own_t, t1, t2)]
    ppermute x9 -> x10, waiting for transfers between devices: 19.7 us -> 19.7 us  [move(): return lax.ppermute(value, AXES, table)]
  transfers between devices with their start and end apart: 10 -> 11, of which waited for: 6 -> 5; matrix products, arithmetic and copies ran while one was open for 0% -> 0% of each run, Pallas kernels for 4% -> 7%
where the time goes in v2:
time: 103 us
  starting transfers between devices  46.7 us (45%)
  waiting for transfers between devices  42.8 us (42%)
  Pallas kernels  10.6 us (10%)
  local copies, waits for them, and re-layouts  1.96 us (2%)
    ppermute x10, starting transfers between devices, move(): return lax.ppermute(value, AXES, table)  37.4 us
    ppermute x1, waiting for transfers between devices, body(): lax.ppermute(code, 'group', [(s, (s + 1) % count) for s in range(count)])  23.1 us
    ppermute x10, waiting for transfers between devices, move(): return lax.ppermute(value, AXES, table)  19.7 us
    ppermute x1, starting transfers between devices, body(): lax.ppermute(code, 'group', [(s, (s + 1) % count) for s in range(count)])  9.31 us
    pallas_call x1, Pallas kernels, body(): image_grad = call(image_kernel, full, [vm] * 4, 0)(own_i, own_t, t1, t2)  2.76 us
    pallas_call x1, Pallas kernels, body(): call(part_kernel, (bf(rows), full), [sm] + [vm] * 5, 60)  2.18 us
  transfers between devices with their start and end apart: 11, of which 5 were waited for; matrix products, arithmetic and copies ran while one was open for 0% of the time, Pallas kernels for 7%

profile of v2, /device:TPU:1, one launch (start us, length us, event | category | flops | bytes accessed | tf_op | source)
XLA Modules:
  0.0 102.9 jit_solution(14769338359363312174)
XLA Ops:
  0.6 1.9 %slice_bitcast_fusion = (bf16[128,1152]{1,0:T(8,128)(2,1)}, bf16[128,1152]{1,0:T(8,128)(2,1)S(1)}) fusion(bf16[1,1,256,1152]{3,2,1,0:T(8,128)(2,1)} %param.2), kind=kLoop, calls=%fused_computation | loop fusion | bytes 1179648 | tf_op jit(solution)/shard_map/slice | solution.py:188
  2.6 1.4 %collective-permute-start = (bf16[128,1152]{1,0:T(8,128)(2,1)S(1)}, bf16[128,1152]{1,0:T(8,128)(2,1)}, u32[]{:S(2)}, u32[]{:S(2)}) collective-permute-start(bf16[128,1152]{1,0:T(8,128)(2,1)S(1)} %get-tuple-element.11), channel_id=1, source_target_pairs={{192,0},{224,160},{193,1},{225,161},{194,2},{226,162},{195,3},{227... | collective-permute-start | bytes 884744 | tf_op jit(solution)/shard_map/ppermute | solution.py:41
  4.0 0.7 collective-permute-start.2
  4.7 1.3 %collective-permute-start.1 = (bf16[128,1152]{1,0:T(8,128)(2,1)S(1)}, bf16[128,1152]{1,0:T(8,128)(2,1)S(1)}, u32[]{:S(2)}, u32[]{:S(2)}) collective-permute-start(bf16[128,1152]{1,0:T(8,128)(2,1)S(1)} %get-tuple-element.13), channel_id=1, source_target_pairs={{192,64},{224,32},{193,65},{225,33},{194,66},{226,34},{195,67},{22... | collective-permute-start | bytes 884744 | tf_op jit(solution)/shard_map/ppermute | solution.py:41
  6.0 9.8 %collective-permute-done.1.after1 = bf16[128,1152]{1,0:T(8,128)(2,1)S(1)} collective-permute-done((bf16[128,1152]{1,0:T(8,128)(2,1)S(1)}, bf16[128,1152]{1,0:T(8,128)(2,1)S(1)}, u32[]{:S(2)}, u32[]{:S(2)}) %collective-permute-start.1) | collective-permute-done | bytes 294944 | tf_op jit(solution)/shard_map/ppermute | solution.py:41
  15.8 0.2 shard_map.41
  16.0 2.3 %collective-permute-start.3 = (bf16[384,1152]{1,0:T(8,128)(2,1)S(1)}, bf16[384,1152]{1,0:T(8,128)(2,1)S(1)}, u32[]{:S(2)}, u32[]{:S(2)}) collective-permute-start(bf16[384,1152]{1,0:T(8,128)(2,1)S(1)} %shard_map.41), channel_id=1, source_target_pairs={{0,64},{32,96},{64,128},{96,160},{128,192},{160,224},{1,65},{33,97... | collective-permute-start | bytes 2654216 | tf_op jit(solution)/shard_map/ppermute | solution.py:41
  18.3 1.9 %collective-permute-start.6 = (bf16[128,1152]{1,0:T(8,128)(2,1)}, bf16[128,1152]{1,0:T(8,128)(2,1)}, u32[]{:S(2)}, u32[]{:S(2)}) collective-permute-start(bf16[128,1152]{1,0:T(8,128)(2,1)} %get-tuple-element.10), channel_id=1, source_target_pairs={{0,64},{32,96},{64,128},{96,160},{128,192},{160,224},{192,256},{22... | collective-permute-start | bytes 884744 | tf_op jit(solution)/shard_map/ppermute | solution.py:41
  20.2 1.3 %collective-permute-start.7 = (bf16[128,1152]{1,0:T(8,128)(2,1)}, bf16[128,1152]{1,0:T(8,128)(2,1)}, u32[]{:S(2)}, u32[]{:S(2)}) collective-permute-start(bf16[128,1152]{1,0:T(8,128)(2,1)} %collective-permute-done.after0), channel_id=1, source_target_pairs={{0,256},{160,288},{1,257},{161,289},{2,258},{162,290},{3,259},{163... | collective-permute-start | bytes 884744 | tf_op jit(solution)/shard_map/ppermute | solution.py:41
  21.5 1.3 %collective-permute-start.5 = (bf16[128,1152]{1,0:T(8,128)(2,1)S(1)}, bf16[128,1152]{1,0:T(8,128)(2,1)}, u32[]{:S(2)}, u32[]{:S(2)}) collective-permute-start(bf16[128,1152]{1,0:T(8,128)(2,1)S(1)} %collective-permute-done.2.after2), channel_id=1, source_target_pairs={{128,256},{96,288},{129,257},{97,289},{130,258},{98,290},{131,259}... | collective-permute-start | bytes 884744 | tf_op jit(solution)/shard_map/ppermute | solution.py:41
  22.8 14.3 %collective-permute-start.4 = (bf16[128,1152]{1,0:T(8,128)(2,1)S(1)}, bf16[128,1152]{1,0:T(8,128)(2,1)}, u32[]{:S(2)}, u32[]{:S(2)}) collective-permute-start(bf16[128,1152]{1,0:T(8,128)(2,1)S(1)} %collective-permute-done.1.after1), channel_id=1, source_target_pairs={{64,256},{32,288},{65,257},{33,289},{66,258},{34,290},{67,259},{35... | collective-permute-start | bytes 884744 | tf_op jit(solution)/shard_map/ppermute | solution.py:41
  37.3 5.3 %collective-permute-done.6.head = bf16[128,1152]{1,0:T(8,128)(2,1)} collective-permute-done((bf16[128,1152]{1,0:T(8,128)(2,1)}, bf16[128,1152]{1,0:T(8,128)(2,1)}, u32[]{:S(2)}, u32[]{:S(2)}) %collective-permute-start.6) | collective-permute-done | bytes 294944 | tf_op jit(solution)/shard_map/ppermute | solution.py:41
  42.6 3.0 %collective-permute-done.7.far0 = bf16[128,1152]{1,0:T(8,128)(2,1)} collective-permute-done((bf16[128,1152]{1,0:T(8,128)(2,1)}, bf16[128,1152]{1,0:T(8,128)(2,1)}, u32[]{:S(2)}, u32[]{:S(2)}) %collective-permute-start.7) | collective-permute-done | bytes 294944 | tf_op jit(solution)/shard_map/ppermute | solution.py:41
  45.5 1.2 %shard_map.42 = (bf16[256,1152]{1,0:T(8,128)(2,1)S(1)}, bf16[256,1152]{1,0:T(8,128)(2,1)S(1)}) custom-call(s32[2]{0:T(128)S(1)} %pad_add_fusion.where, bf16[128,1152]{1,0:T(8,128)(2,1)} %collective-permute-done.6.head, bf16[384,1152]{1,0:T(8,128)(2,1)S(1)} %collective-permute-done.3.rest, bf16[128,1152]{1,0:T(8,128)(2,1)} %collective-permute-done.7.far0, ...), custom_call_target="tpu_custom_call" | custom-call | bytes 2097152 | tf_op jit(solution)/shard_map/pallas_call | solution.py:194
  46.7 9.3 %collective-permute-start.8 = (bf16[256,1152]{1,0:T(8,128)(2,1)S(1)}, bf16[256,1152]{1,0:T(8,128)(2,1)S(1)}, u32[]{:S(2)}, u32[]{:S(2)}) collective-permute-start(bf16[256,1152]{1,0:T(8,128)(2,1)S(1)} %get-tuple-element.8), channel_id=1, source_target_pairs={{0,32},{32,0},{64,96},{96,64},{128,160},{160,128},{192,224},{224,1... | collective-permute-start | bytes 1769480 | tf_op jit(solution)/shard_map/ppermute | solution.py:41
  56.1 2.2 %shard_map.43 = (bf16[256,1152]{1,0:T(8,128)(2,1)S(1)}, f32[256,1152]{1,0:T(8,128)S(1)}) custom-call(s32[2]{0:T(128)S(1)} %pad_add_fusion.where, bf16[384,1152]{1,0:T(8,128)(2,1)S(1)} %collective-permute-done.3.rest, bf16[128,1152]{1,0:T(8,128)(2,1)} %collective-permute-done.4.far1, bf16[128,1152]{1,0:T(8,128)(2,1)} %collective-permute-done.5.far2, ...), custom_call_target="tpu_custom_call" | custom-call | flops 18119393280 | bytes 2097152 | tf_op jit(solution)/shard_map/pallas_call | solution.py:196
  58.3 1.7 %shard_map.44.code = bf16[272,1152]{1,0:T(8,128)(2,1)S(1)} custom-call(f32[256,1152]{1,0:T(8,128)S(1)} %get-tuple-element.7.part, bf16[256,1152]{1,0:T(8,128)(2,1)S(1)} %collective-permute-done.8.i1, bf16[256,1152]{1,0:T(8,128)(2,1)S(1)} %get-tuple-element.9.t2), custom_call_target="tpu_custom_call" | custom-call | flops 301989888 | bytes 2097152 | tf_op jit(solution)/shard_map/pallas_call | solution.py:197
  59.9 9.3 %collective-permute-start.10 = (bf16[272,1152]{1,0:T(8,128)(2,1)S(1)}, bf16[272,1152]{1,0:T(8,128)(2,1)S(1)}, u32[]{:S(2)}, u32[]{:S(2)}) collective-permute-start(bf16[272,1152]{1,0:T(8,128)(2,1)S(1)} %shard_map.44.code), channel_id=1, source_target_pairs={{0,1},{1,2},{2,3},{3,4},{4,5},{5,6},{6,7},{7,8},{8,9},{9,10},{10,1... | collective-permute-start | bytes 1880072 | tf_op jit(solution)/shard_map/ppermute | solution.py:199
  69.2 0.6 shard_map.45
  69.9 3.6 %collective-permute-start.9 = (bf16[256,1152]{1,0:T(8,128)(2,1)S(1)}, bf16[256,1152]{1,0:T(8,128)(2,1)S(1)}, u32[]{:S(2)}, u32[]{:S(2)}) collective-permute-start(bf16[256,1152]{1,0:T(8,128)(2,1)S(1)} %shard_map.45), channel_id=1, source_target_pairs={{0,32},{32,0},{64,96},{96,64},{128,160},{160,128},{192,224},{224,1... | collective-permute-start | bytes 1769480 | tf_op jit(solution)/shard_map/ppermute | solution.py:41
  73.4 1.6 %collective-permute-done.9.t1 = bf16[256,1152]{1,0:T(8,128)(2,1)S(1)} collective-permute-done((bf16[256,1152]{1,0:T(8,128)(2,1)S(1)}, bf16[256,1152]{1,0:T(8,128)(2,1)S(1)}, u32[]{:S(2)}, u32[]{:S(2)}) %collective-permute-start.9) | collective-permute-done | bytes 589856 | tf_op jit(solution)/shard_map/ppermute | solution.py:41
  75.0 2.8 %shard_map.46 = f32[256,1152]{1,0:T(8,128)} custom-call(bf16[256,1152]{1,0:T(8,128)(2,1)S(1)} %bitcast.17, bf16[256,1152]{1,0:T(8,128)(2,1)S(1)} %bitcast.20, bf16[256,1152]{1,0:T(8,128)(2,1)S(1)} %collective-permute-done.9.t1, bf16[256,1152]{1,0:T(8,128)(2,1)S(1)} %get-tuple-element.9.t2), custom_call_target="tpu_custom_call" | custom-call | bytes 2097152 | tf_op jit(solution)/shard_map/pallas_call | solution.py:201
  77.8 23.1 %collective-permute-done.10.code = bf16[272,1152]{1,0:T(8,128)(2,1)S(1)} collective-permute-done((bf16[272,1152]{1,0:T(8,128)(2,1)S(1)}, bf16[272,1152]{1,0:T(8,128)(2,1)S(1)}, u32[]{:S(2)}, u32[]{:S(2)}) %collective-permute-start.10) | collective-permute-done | bytes 626720 | tf_op jit(solution)/shard_map/ppermute | solution.py:199
  100.9 2.0 %shard_map.47 = f32[256,1152]{1,0:T(8,128)} custom-call(bf16[272,1152]{1,0:T(8,128)(2,1)S(1)} %collective-permute-done.10.code), custom_call_target="tpu_custom_call" | custom-call | bytes 2097152 | tf_op jit(solution)/shard_map/pallas_call | solution.py:203
  (12 shorter events, 0.1 us)
Async XLA Ops:
  0.6 15.2 %copy-start = (bf16[1,1,256,1152]{3,2,1,0:T(8,128)(2,1)S(1)}, bf16[1,1,256,1152]{3,2,1,0:T(8,128)(2,1)}, u32[]{:S(2)}) copy-start(bf16[1,1,256,1152]{3,2,1,0:T(8,128)(2,1)} %param.2) | copy-start | bytes 1769476
  0.6 3.3 %copy-start.1 = (bf16[1,1,256,1152]{3,2,1,0:T(8,128)(2,1)S(1)}, bf16[1,1,256,1152]{3,2,1,0:T(8,128)(2,1)}, u32[]{:S(2)}) copy-start(bf16[1,1,256,1152]{3,2,1,0:T(8,128)(2,1)} %param.3) | copy-start | bytes 1769476
  2.6 3.4 %collective-permute-start = (bf16[128,1152]{1,0:T(8,128)(2,1)S(1)}, bf16[128,1152]{1,0:T(8,128)(2,1)}, u32[]{:S(2)}, u32[]{:S(2)}) collective-permute-start(bf16[128,1152]{1,0:T(8,128)(2,1)S(1)} %get-tuple-element.11), channel_id=1, source_target_pairs={{192,0},{224,160},{193,1},{225,161},{194,2},{226,162},{195,3},{227... | collective-permute-start | bytes 884744 | tf_op jit(solution)/shard_map/ppermute | solution.py:41
  4.0 2.0 %collective-permute-start.2 = (bf16[128,1152]{1,0:T(8,128)(2,1)S(1)}, bf16[128,1152]{1,0:T(8,128)(2,1)S(1)}, u32[]{:S(2)}, u32[]{:S(2)}) collective-permute-start(bf16[128,1152]{1,0:T(8,128)(2,1)S(1)} %get-tuple-element.12), channel_id=1, source_target_pairs={{192,128},{224,96},{193,129},{225,97},{194,130},{226,98},{195,131}... | collective-permute-start | bytes 884744 | tf_op jit(solution)/shard_map/ppermute | solution.py:41
  4.7 11.1 %collective-permute-start.1 = (bf16[128,1152]{1,0:T(8,128)(2,1)S(1)}, bf16[128,1152]{1,0:T(8,128)(2,1)S(1)}, u32[]{:S(2)}, u32[]{:S(2)}) collective-permute-start(bf16[128,1152]{1,0:T(8,128)(2,1)S(1)} %get-tuple-element.13), channel_id=1, source_target_pairs={{192,64},{224,32},{193,65},{225,33},{194,66},{226,34},{195,67},{22... | collective-permute-start | bytes 884744 | tf_op jit(solution)/shard_map/ppermute | solution.py:41
  16.0 29.6 %collective-permute-start.3 = (bf16[384,1152]{1,0:T(8,128)(2,1)S(1)}, bf16[384,1152]{1,0:T(8,128)(2,1)S(1)}, u32[]{:S(2)}, u32[]{:S(2)}) collective-permute-start(bf16[384,1152]{1,0:T(8,128)(2,1)S(1)} %shard_map.41), channel_id=1, source_target_pairs={{0,64},{32,96},{64,128},{96,160},{128,192},{160,224},{1,65},{33,97... | collective-permute-start | bytes 2654216 | tf_op jit(solution)/shard_map/ppermute | solution.py:41
  18.3 24.3 %collective-permute-start.6 = (bf16[128,1152]{1,0:T(8,128)(2,1)}, bf16[128,1152]{1,0:T(8,128)(2,1)}, u32[]{:S(2)}, u32[]{:S(2)}) collective-permute-start(bf16[128,1152]{1,0:T(8,128)(2,1)} %get-tuple-element.10), channel_id=1, source_target_pairs={{0,64},{32,96},{64,128},{96,160},{128,192},{160,224},{192,256},{22... | collective-permute-start | bytes 884744 | tf_op jit(solution)/shard_map/ppermute | solution.py:41
  20.2 25.3 %collective-permute-start.7 = (bf16[128,1152]{1,0:T(8,128)(2,1)}, bf16[128,1152]{1,0:T(8,128)(2,1)}, u32[]{:S(2)}, u32[]{:S(2)}) collective-permute-start(bf16[128,1152]{1,0:T(8,128)(2,1)} %collective-permute-done.after0), channel_id=1, source_target_pairs={{0,256},{160,288},{1,257},{161,289},{2,258},{162,290},{3,259},{163... | collective-permute-start | bytes 884744 | tf_op jit(solution)/shard_map/ppermute | solution.py:41
  21.5 34.5 %collective-permute-start.5 = (bf16[128,1152]{1,0:T(8,128)(2,1)S(1)}, bf16[128,1152]{1,0:T(8,128)(2,1)}, u32[]{:S(2)}, u32[]{:S(2)}) collective-permute-start(bf16[128,1152]{1,0:T(8,128)(2,1)S(1)} %collective-permute-done.2.after2), channel_id=1, source_target_pairs={{128,256},{96,288},{129,257},{97,289},{130,258},{98,290},{131,259}... | collective-permute-start | bytes 884744 | tf_op jit(solution)/shard_map/ppermute | solution.py:41
  22.8 33.2 %collective-permute-start.4 = (bf16[128,1152]{1,0:T(8,128)(2,1)S(1)}, bf16[128,1152]{1,0:T(8,128)(2,1)}, u32[]{:S(2)}, u32[]{:S(2)}) collective-permute-start(bf16[128,1152]{1,0:T(8,128)(2,1)S(1)} %collective-permute-done.1.after1), channel_id=1, source_target_pairs={{64,256},{32,288},{65,257},{33,289},{66,258},{34,290},{67,259},{35... | collective-permute-start | bytes 884744 | tf_op jit(solution)/shard_map/ppermute | solution.py:41
  46.7 11.5 %collective-permute-start.8 = (bf16[256,1152]{1,0:T(8,128)(2,1)S(1)}, bf16[256,1152]{1,0:T(8,128)(2,1)S(1)}, u32[]{:S(2)}, u32[]{:S(2)}) collective-permute-start(bf16[256,1152]{1,0:T(8,128)(2,1)S(1)} %get-tuple-element.8), channel_id=1, source_target_pairs={{0,32},{32,0},{64,96},{96,64},{128,160},{160,128},{192,224},{224,1... | collective-permute-start | bytes 1769480 | tf_op jit(solution)/shard_map/ppermute | solution.py:41
  59.9 41.0 %collective-permute-start.10 = (bf16[272,1152]{1,0:T(8,128)(2,1)S(1)}, bf16[272,1152]{1,0:T(8,128)(2,1)S(1)}, u32[]{:S(2)}, u32[]{:S(2)}) collective-permute-start(bf16[272,1152]{1,0:T(8,128)(2,1)S(1)} %shard_map.44.code), channel_id=1, source_target_pairs={{0,1},{1,2},{2,3},{3,4},{4,5},{5,6},{6,7},{7,8},{8,9},{9,10},{10,1... | collective-permute-start | bytes 1880072 | tf_op jit(solution)/shard_map/ppermute | solution.py:199
  69.9 5.2 %collective-permute-start.9 = (bf16[256,1152]{1,0:T(8,128)(2,1)S(1)}, bf16[256,1152]{1,0:T(8,128)(2,1)S(1)}, u32[]{:S(2)}, u32[]{:S(2)}) collective-permute-start(bf16[256,1152]{1,0:T(8,128)(2,1)S(1)} %shard_map.45), channel_id=1, source_target_pairs={{0,32},{32,0},{64,96},{96,64},{128,160},{160,128},{192,224},{224,1... | collective-permute-start | bytes 1769480 | tf_op jit(solution)/shard_map/ppermute | solution.py:41

commit v3 on v2

--- a/solution.py
+++ b/solution.py
@@ -28,13 +28,13 @@
 
 
 PLANES = ((0, 2), (1, 0), (2, 1))
-NEAR = [((x, c), (x + 1, 0, c)) for x in range(3) for c in range(2)]
-STRAIGHT = [((3, c), (0, 4, c)) for c in range(2)]
-MOVE_ALL = pairs(*NEAR, *STRAIGHT)
-MOVE_NEAR = pairs(*NEAR)
-MOVE_OUT = [pairs(*(((3, c), (p[c], 0, c)) for c in range(2))) for p in PLANES]
-MOVE_ON = [pairs(*(((p[c], c), (0, 4, c)) for c in range(2))) for p in PLANES]
-MOVE_SWAP = pairs(*(((x, c), (x, 0, 1 - c)) for x in range(4) for c in range(2)))
+CORES = range(2)
+MOVE_ALL = pairs(*(((x, c), (x + 1, 0, c)) for x in range(3) for c in CORES), *(((3, c), (0, 4, c)) for c in CORES))
+MOVE_OUT = [pairs(*(m for c in CORES for m in (((3, c), (p[c], 0, c)), ((p[c], c), (p[c] + 1, 0, c))))) for p in PLANES]
+MOVE_ON = [
+    pairs(*(((x, c), (0, 4, c) if x == p[c] else (x + 1, 0, c)) for x in range(3) for c in CORES)) for p in PLANES
+]
+MOVE_SWAP = pairs(*(((x, c), (x, 0, 1 - c)) for x in range(4) for c in CORES))
 
 
 def move(value, table):
@@ -58,52 +58,31 @@
     return out.astype(jnp.bfloat16)
 
 
-def near_kernel(images, texts, after0, after1, after2, rest, sems):
-    half = after0.shape[0]
-    high = pl.ds(half, half)
-    copies = [
-        pltpu.make_async_copy(images.at[high], rest.at[pl.ds(0, half)], sems.at[0]),
-        pltpu.make_async_copy(texts, rest.at[pl.ds(half, 2 * half)], sems.at[1]),
-    ]
-    for copy in copies:
-        copy.start()
-    for copy in copies:
-        copy.wait()
+def choose(flag, a, b, out):
+    @pl.when(flag == 1)
+    def _():
+        out[...] = a[...]
+
+    @pl.when(flag == 0)
+    def _():
+        out[...] = b[...]
 
 
-def pick_images(where, head, rest, far0, i0, i2, swap):
+def relay_kernel(relay, out, own, sent):
+    choose(relay[0], out, own, sent)
+
+
+def pick_images(where, head, out0, far0, i0, i2, swap):
     half = head.shape[0]
     i2[:half] = head[...]
-
-    @pl.when(where[0] == 1)
-    def _():
-        i2[half:] = far0[...]
-
-    @pl.when(where[0] == 0)
-    def _():
-        i2[half:] = rest[:half]
-
-    @pl.when(where[1] == 1)
-    def _():
-        swap[...] = i2[...]
-
-    @pl.when(where[1] == 0)
-    def _():
-        swap[...] = i0[...]
+    choose(where[1], out0, far0, i2.at[half:])
+    choose(where[0], i2, i0, swap)
 
 
-def part_kernel(where, rest, far1, far2, i2, i0, t2, out):
+def part_kernel(where, out1, far1, out2, far2, i2, i0, t2, out):
     half = far1.shape[0]
-
-    @pl.when(where[0] == 1)
-    def _():
-        t2[:half] = far1[...]
-        t2[half:] = far2[...]
-
-    @pl.when(where[0] == 0)
-    def _():
-        t2[...] = rest[half:]
-
+    choose(where[2], out1, far1, t2.at[:half])
+    choose(where[3], out2, far2, t2.at[half:])
     text = t2[...]
     out[...] = dot_tn(coefs(i2[...], text, True), i2[...]) + dot_tn(coefs(i0[...], text, False), i0[...])
 
@@ -121,13 +100,7 @@
 
 
 def pick_texts(where, code, t2, t0, swap):
-    @pl.when(where[1] == 1)
-    def _():
-        swap[...] = t2[...]
-
-    @pl.when(where[1] == 0)
-    def _():
-        swap[...] = t0[...]
+    choose(where[0], t2, t0, swap)
 
 
 def read_kernel(code, out):
@@ -158,8 +131,9 @@
     own_t = texts.reshape(rows, width)
     blk = lax.axis_index("blk")
     core = blk % 2
-    first = (blk // 2) % 4 == 0
-    where = jnp.stack([first.astype(jnp.int32), core.astype(jnp.int32)])
+    x = (blk // 2) % 4
+    plane = [jnp.where(core == 0, *p) for p in PLANES]
+    where = jnp.stack([core] + [(x == p + 1).astype(jnp.int32) for p in plane])
 
     vm = pl.BlockSpec(memory_space=pltpu.VMEM)
     sm = pl.BlockSpec(memory_space=pltpu.SMEM)
@@ -184,16 +158,18 @@
 
     full = jax.ShapeDtypeStruct((rows, width), jnp.float32)
 
-    out = [move(p, t) for p, t in zip((own_i[half:], own_t[:half], own_t[half:]), MOVE_OUT)]
+    pieces = (own_i[half:], own_t[:half], own_t[half:])
+    out = [move(p, t) for p, t in zip(pieces, MOVE_OUT)]
     head = move(own_i[:half], MOVE_ALL)
-    near = call(
-        near_kernel, bf(3 * half), [anywhere] * 5, 0, scratch=[pltpu.SemaphoreType.DMA((2,))]
-    )(own_i, own_t, *out)
-    rest = move(near, MOVE_NEAR)
-    far = [move(p, t) for p, t in zip(out, MOVE_ON)]
-    i2, swap_i = call(pick_images, (bf(rows),) * 2, [sm] + [vm] * 4, 0)(where, head, rest, far[0], own_i)
+    far = []
+    for q, o, p, t in zip(plane, out, pieces, MOVE_ON):
+        relay = (x == q).astype(jnp.int32).reshape(1)
+        far.append(move(call(relay_kernel, bf(half), [sm] + [vm] * 2, 0)(relay, o, p), t))
+    i2, swap_i = call(pick_images, (bf(rows),) * 2, [sm] + [vm] * 4, 0)(where, head, out[0], far[0], own_i)
     i1 = move(swap_i, MOVE_SWAP)
-    t2, part = call(part_kernel, (bf(rows), full), [sm] + [vm] * 5, 60)(where, rest, far[1], far[2], i2, own_i)
+    t2, part = call(part_kernel, (bf(rows), full), [sm] + [vm] * 6, 60)(
+        where, out[1], far[1], out[2], far[2], i2, own_i
+    )
     code = call(text_kernel, bf(rows + EXTRA), [vm] * 3, 1)(part, i1, t2)
     count = lax.axis_size("group")
     got = lax.ppermute(code, "group", [(s, (s + 1) % count) for s in range(count)])

time: 103 us -> 95.9 us (0.931)
  waiting for transfers between devices: 42.8 us -> 26.4 us
  starting transfers between devices: 46.7 us -> 55.8 us
    ppermute x1, waiting for transfers between devices: 23.1 us -> 14.7 us  [body(): lax.ppermute(code, 'group', [(s, (s + 1) % count) for s in range(count)])]
    ppermute x10 -> x9, starting transfers between devices: 37.4 us -> 45.7 us  [move(): return lax.ppermute(value, AXES, table)]
    ppermute x10 -> x9, waiting for transfers between devices: 19.7 us -> 11.7 us  [move(): return lax.ppermute(value, AXES, table)]
    pallas_call x2 -> x4, Pallas kernels: 2.38 us -> 2.27 us  [the longest x1 2.17 us: body(): call(part_kernel, (bf(rows), full), [sm] + [vm] * 6, 60)]
  transfers between devices with their start and end apart: 11 -> 10, of which waited for: 5 -> 5; matrix products, arithmetic and copies ran while one was open for 0% -> 0% of each run, Pallas kernels for 7% -> 7%
where the time goes in v3:
time: 95.9 us; the launch traced here: 95.5 us
  starting transfers between devices  55.8 us (58%)
  waiting for transfers between devices  26.4 us (28%)
  Pallas kernels  10.4 us (11%)
  local copies, waits for them, and re-layouts  1.93 us (2%)
    ppermute x9, starting transfers between devices, move(): return lax.ppermute(value, AXES, table)  45.7 us
    ppermute x1, waiting for transfers between devices, body(): lax.ppermute(code, 'group', [(s, (s + 1) % count) for s in range(count)])  14.7 us
    ppermute x9, waiting for transfers between devices, move(): return lax.ppermute(value, AXES, table)  11.7 us
    ppermute x1, starting transfers between devices, body(): lax.ppermute(code, 'group', [(s, (s + 1) % count) for s in range(count)])  10.1 us
    pallas_call x1, Pallas kernels, body(): image_grad = call(image_kernel, full, [vm] * 4, 0)(own_i, own_t, t1, t2)  2.76 us
    pallas_call x1, Pallas kernels, body(): call(part_kernel, (bf(rows), full), [sm] + [vm] * 6, 60)  2.17 us
    pallas_call x1, Pallas kernels, body(): call(read_kernel, full, [vm], 0, out_specs=pl.BlockSpec((cut, width), lam...  2.03 us
    slice x2, local copies, waits for them, and re-layouts, body(): pieces = (own_i[half:], own_t[:half], own_t[half:])  1.92 us
  transfers between devices with their start and end apart: 10, of which 5 were waited for; matrix products, arithmetic and copies ran while one was open for 0% of the time, Pallas kernels for 7%

profile of v3, /device:TPU:1, one launch (start us, length us, event | category | flops | bytes accessed | tf_op | source)
XLA Modules:
  0.0 95.5 jit_solution(8307154033078646363)
XLA Ops:
  0.6 1.9 %slice_bitcast_fusion = (bf16[128,1152]{1,0:T(8,128)(2,1)S(1)}, bf16[128,1152]{1,0:T(8,128)(2,1)}) fusion(bf16[1,1,256,1152]{3,2,1,0:T(8,128)(2,1)} %param.2), kind=kLoop, calls=%fused_computation | loop fusion | bytes 1179648 | tf_op jit(solution)/shard_map/slice | solution.py:161
  2.5 0.7 collective-permute-start.5
  3.3 0.7 collective-permute-start.2
  3.9 8.5 %collective-permute-start = (bf16[128,1152]{1,0:T(8,128)(2,1)S(1)}, bf16[128,1152]{1,0:T(8,128)(2,1)S(1)}, u32[]{:S(2)}, u32[]{:S(2)}) collective-permute-start(bf16[128,1152]{1,0:T(8,128)(2,1)S(1)} %get-tuple-element.13.own), channel_id=1, source_target_pairs={{192,64},{64,128},{224,32},{32,96},{193,65},{65,129},{225,33},{33,... | collective-permute-start | bytes 884744 | tf_op jit(solution)/shard_map/ppermute | solution.py:41
  12.5 1.9 %collective-permute-start.4 = (bf16[128,1152]{1,0:T(8,128)(2,1)}, bf16[128,1152]{1,0:T(8,128)(2,1)S(1)}, u32[]{:S(2)}, u32[]{:S(2)}) collective-permute-start(bf16[128,1152]{1,0:T(8,128)(2,1)} %get-tuple-element.11), channel_id=1, source_target_pairs={{0,64},{32,96},{64,128},{96,160},{128,192},{160,224},{192,256},{22... | collective-permute-start | bytes 884744 | tf_op jit(solution)/shard_map/ppermute | solution.py:41
  14.5 0.0 copy-start
  14.5 2.1 %collective-permute-start.6 = (bf16[128,1152]{1,0:T(8,128)(2,1)S(1)}, bf16[128,1152]{1,0:T(8,128)(2,1)}, u32[]{:S(2)}, u32[]{:S(2)}) collective-permute-start(bf16[128,1152]{1,0:T(8,128)(2,1)S(1)} %shard_map.43), channel_id=1, source_target_pairs={{0,256},{32,96},{64,128},{96,160},{128,192},{160,288},{1,257},{33,... | collective-permute-start | bytes 884744 | tf_op jit(solution)/shard_map/ppermute | solution.py:41
  16.6 1.9 %collective-permute-start.3 = (bf16[128,1152]{1,0:T(8,128)(2,1)S(1)}, bf16[128,1152]{1,0:T(8,128)(2,1)}, u32[]{:S(2)}, u32[]{:S(2)}) collective-permute-start(bf16[128,1152]{1,0:T(8,128)(2,1)S(1)} %shard_map.42), channel_id=1, source_target_pairs={{0,64},{32,96},{64,128},{96,288},{128,256},{160,224},{1,65},{33,97... | collective-permute-start | bytes 884744 | tf_op jit(solution)/shard_map/ppermute | solution.py:41
  18.6 13.9 %collective-permute-start.1 = (bf16[128,1152]{1,0:T(8,128)(2,1)S(1)}, bf16[128,1152]{1,0:T(8,128)(2,1)}, u32[]{:S(2)}, u32[]{:S(2)}) collective-permute-start(bf16[128,1152]{1,0:T(8,128)(2,1)S(1)} %shard_map.41), channel_id=1, source_target_pairs={{0,64},{32,288},{64,256},{96,160},{128,192},{160,224},{1,65},{33,2... | collective-permute-start | bytes 884744 | tf_op jit(solution)/shard_map/ppermute | solution.py:41
  32.5 0.1 pad_add_fusion.where
  32.6 3.9 %collective-permute-done.4.head = bf16[128,1152]{1,0:T(8,128)(2,1)S(1)} collective-permute-done((bf16[128,1152]{1,0:T(8,128)(2,1)}, bf16[128,1152]{1,0:T(8,128)(2,1)S(1)}, u32[]{:S(2)}, u32[]{:S(2)}) %collective-permute-start.4) | collective-permute-done | bytes 294944 | tf_op jit(solution)/shard_map/ppermute | solution.py:41
  36.5 3.2 %collective-permute-done.6.far0 = bf16[128,1152]{1,0:T(8,128)(2,1)} collective-permute-done((bf16[128,1152]{1,0:T(8,128)(2,1)S(1)}, bf16[128,1152]{1,0:T(8,128)(2,1)}, u32[]{:S(2)}, u32[]{:S(2)}) %collective-permute-start.6) | collective-permute-done | bytes 294944 | tf_op jit(solution)/shard_map/ppermute | solution.py:41
  39.6 1.1 %shard_map.44 = (bf16[256,1152]{1,0:T(8,128)(2,1)S(1)}, bf16[256,1152]{1,0:T(8,128)(2,1)S(1)}) custom-call(s32[4]{0:T(128)S(1)} %pad_add_fusion.where, bf16[128,1152]{1,0:T(8,128)(2,1)S(1)} %collective-permute-done.4.head, bf16[128,1152]{1,0:T(8,128)(2,1)S(1)} %collective-permute-done.5.out.out0, bf16[128,1152]{1,0:T(8,128)(2,1)} %collective-permute-done.6.far0, ...), custom_call_target="tpu_custom_call" | custom-call | bytes 2097152 | tf_op jit(solution)/shard_map/pallas_call | solution.py:168
  40.7 5.1 %collective-permute-start.7 = (bf16[256,1152]{1,0:T(8,128)(2,1)S(1)}, bf16[256,1152]{1,0:T(8,128)(2,1)S(1)}, u32[]{:S(2)}, u32[]{:S(2)}) collective-permute-start(bf16[256,1152]{1,0:T(8,128)(2,1)S(1)} %get-tuple-element.8), channel_id=1, source_target_pairs={{0,32},{32,0},{64,96},{96,64},{128,160},{160,128},{192,224},{224,1... | collective-permute-start | bytes 1769480 | tf_op jit(solution)/shard_map/ppermute | solution.py:41
  45.8 3.1 %collective-permute-done.1.far1 = bf16[128,1152]{1,0:T(8,128)(2,1)} collective-permute-done((bf16[128,1152]{1,0:T(8,128)(2,1)S(1)}, bf16[128,1152]{1,0:T(8,128)(2,1)}, u32[]{:S(2)}, u32[]{:S(2)}) %collective-permute-start.1) | collective-permute-done | bytes 294944 | tf_op jit(solution)/shard_map/ppermute | solution.py:41
  48.9 2.2 %shard_map.45 = (bf16[256,1152]{1,0:T(8,128)(2,1)S(1)}, f32[256,1152]{1,0:T(8,128)S(1)}) custom-call(s32[4]{0:T(128)S(1)} %pad_add_fusion.where, bf16[128,1152]{1,0:T(8,128)(2,1)S(1)} %collective-permute-done.out.out1, bf16[128,1152]{1,0:T(8,128)(2,1)} %collective-permute-done.1.far1, bf16[128,1152]{1,0:T(8,128)(2,1)S(1)} %collective-permute-done.2.out.out2, ...), custom_call_target="tpu_custom_call" | custom-call | flops 18119393280 | bytes 2097152 | tf_op jit(solution)/shard_map/pallas_call | solution.py:170
  51.1 1.7 %shard_map.46.code = bf16[272,1152]{1,0:T(8,128)(2,1)S(1)} custom-call(f32[256,1152]{1,0:T(8,128)S(1)} %get-tuple-element.7.part, bf16[256,1152]{1,0:T(8,128)(2,1)S(1)} %collective-permute-done.7.i1, bf16[256,1152]{1,0:T(8,128)(2,1)S(1)} %get-tuple-element.9.t2), custom_call_target="tpu_custom_call" | custom-call | flops 301989888 | bytes 2097152 | tf_op jit(solution)/shard_map/pallas_call | solution.py:173
  52.8 10.1 %collective-permute-start.9 = (bf16[272,1152]{1,0:T(8,128)(2,1)S(1)}, bf16[272,1152]{1,0:T(8,128)(2,1)S(1)}, u32[]{:S(2)}, u32[]{:S(2)}) collective-permute-start(bf16[272,1152]{1,0:T(8,128)(2,1)S(1)} %shard_map.46.code), channel_id=1, source_target_pairs={{0,1},{1,2},{2,3},{3,4},{4,5},{5,6},{6,7},{7,8},{8,9},{9,10},{10,1... | collective-permute-start | bytes 1880072 | tf_op jit(solution)/shard_map/ppermute | solution.py:175
  62.9 0.6 shard_map.47
  63.5 10.9 %collective-permute-start.8 = (bf16[256,1152]{1,0:T(8,128)(2,1)S(1)}, bf16[256,1152]{1,0:T(8,128)(2,1)S(1)}, u32[]{:S(2)}, u32[]{:S(2)}) collective-permute-start(bf16[256,1152]{1,0:T(8,128)(2,1)S(1)} %shard_map.47), channel_id=1, source_target_pairs={{0,32},{32,0},{64,96},{96,64},{128,160},{160,128},{192,224},{224,1... | collective-permute-start | bytes 1769480 | tf_op jit(solution)/shard_map/ppermute | solution.py:41
  74.4 1.6 %collective-permute-done.8.t1 = bf16[256,1152]{1,0:T(8,128)(2,1)S(1)} collective-permute-done((bf16[256,1152]{1,0:T(8,128)(2,1)S(1)}, bf16[256,1152]{1,0:T(8,128)(2,1)S(1)}, u32[]{:S(2)}, u32[]{:S(2)}) %collective-permute-start.8) | collective-permute-done | bytes 589856 | tf_op jit(solution)/shard_map/ppermute | solution.py:41
  76.0 2.8 %shard_map.48 = f32[256,1152]{1,0:T(8,128)} custom-call(bf16[256,1152]{1,0:T(8,128)(2,1)S(1)} %bitcast.21, bf16[256,1152]{1,0:T(8,128)(2,1)S(1)} %bitcast.23, bf16[256,1152]{1,0:T(8,128)(2,1)S(1)} %collective-permute-done.8.t1, bf16[256,1152]{1,0:T(8,128)(2,1)S(1)} %get-tuple-element.9.t2), custom_call_target="tpu_custom_call" | custom-call | bytes 2097152 | tf_op jit(solution)/shard_map/pallas_call | solution.py:177
  78.8 14.7 %collective-permute-done.9.code = bf16[272,1152]{1,0:T(8,128)(2,1)S(1)} collective-permute-done((bf16[272,1152]{1,0:T(8,128)(2,1)S(1)}, bf16[272,1152]{1,0:T(8,128)(2,1)S(1)}, u32[]{:S(2)}, u32[]{:S(2)}) %collective-permute-start.9) | collective-permute-done | bytes 626720 | tf_op jit(solution)/shard_map/ppermute | solution.py:175
  93.4 2.0 %shard_map.49 = f32[256,1152]{1,0:T(8,128)} custom-call(bf16[272,1152]{1,0:T(8,128)(2,1)S(1)} %collective-permute-done.9.code), custom_call_target="tpu_custom_call" | custom-call | bytes 2097152 | tf_op jit(solution)/shard_map/pallas_call | solution.py:179
  (12 shorter events, 0.2 us)
Async XLA Ops:
  0.6 2.6 %copy-start.1 = (bf16[1,1,256,1152]{3,2,1,0:T(8,128)(2,1)S(1)}, bf16[1,1,256,1152]{3,2,1,0:T(8,128)(2,1)}, u32[]{:S(2)}) copy-start(bf16[1,1,256,1152]{3,2,1,0:T(8,128)(2,1)} %param.3) | copy-start | bytes 1769476
  2.5 12.0 %collective-permute-start.5 = (bf16[128,1152]{1,0:T(8,128)(2,1)S(1)}, bf16[128,1152]{1,0:T(8,128)(2,1)S(1)}, u32[]{:S(2)}, u32[]{:S(2)}) collective-permute-start(bf16[128,1152]{1,0:T(8,128)(2,1)S(1)} %get-tuple-element.10.own), channel_id=1, source_target_pairs={{192,0},{0,64},{224,160},{160,224},{193,1},{1,65},{225,161},{161,2... | collective-permute-start | bytes 884744 | tf_op jit(solution)/shard_map/ppermute | solution.py:41
  3.3 13.3 %collective-permute-start.2 = (bf16[128,1152]{1,0:T(8,128)(2,1)S(1)}, bf16[128,1152]{1,0:T(8,128)(2,1)S(1)}, u32[]{:S(2)}, u32[]{:S(2)}) collective-permute-start(bf16[128,1152]{1,0:T(8,128)(2,1)S(1)} %get-tuple-element.12.own), channel_id=1, source_target_pairs={{192,128},{128,192},{224,96},{96,160},{193,129},{129,193},{225,97}... | collective-permute-start | bytes 884744 | tf_op jit(solution)/shard_map/ppermute | solution.py:41
  3.9 14.6 %collective-permute-start = (bf16[128,1152]{1,0:T(8,128)(2,1)S(1)}, bf16[128,1152]{1,0:T(8,128)(2,1)S(1)}, u32[]{:S(2)}, u32[]{:S(2)}) collective-permute-start(bf16[128,1152]{1,0:T(8,128)(2,1)S(1)} %get-tuple-element.13.own), channel_id=1, source_target_pairs={{192,64},{64,128},{224,32},{32,96},{193,65},{65,129},{225,33},{33,... | collective-permute-start | bytes 884744 | tf_op jit(solution)/shard_map/ppermute | solution.py:41
  12.5 24.0 %collective-permute-start.4 = (bf16[128,1152]{1,0:T(8,128)(2,1)}, bf16[128,1152]{1,0:T(8,128)(2,1)S(1)}, u32[]{:S(2)}, u32[]{:S(2)}) collective-permute-start(bf16[128,1152]{1,0:T(8,128)(2,1)} %get-tuple-element.11), channel_id=1, source_target_pairs={{0,64},{32,96},{64,128},{96,160},{128,192},{160,224},{192,256},{22... | collective-permute-start | bytes 884744 | tf_op jit(solution)/shard_map/ppermute | solution.py:41
  14.5 25.2 %copy-start = (bf16[1,1,256,1152]{3,2,1,0:T(8,128)(2,1)S(1)}, bf16[1,1,256,1152]{3,2,1,0:T(8,128)(2,1)}, u32[]{:S(2)}) copy-start(bf16[1,1,256,1152]{3,2,1,0:T(8,128)(2,1)} %param.2) | copy-start | bytes 1769476
  14.5 25.1 %collective-permute-start.6 = (bf16[128,1152]{1,0:T(8,128)(2,1)S(1)}, bf16[128,1152]{1,0:T(8,128)(2,1)}, u32[]{:S(2)}, u32[]{:S(2)}) collective-permute-start(bf16[128,1152]{1,0:T(8,128)(2,1)S(1)} %shard_map.43), channel_id=1, source_target_pairs={{0,256},{32,96},{64,128},{96,160},{128,192},{160,288},{1,257},{33,... | collective-permute-start | bytes 884744 | tf_op jit(solution)/shard_map/ppermute | solution.py:41
  16.6 29.2 %collective-permute-start.3 = (bf16[128,1152]{1,0:T(8,128)(2,1)S(1)}, bf16[128,1152]{1,0:T(8,128)(2,1)}, u32[]{:S(2)}, u32[]{:S(2)}) collective-permute-start(bf16[128,1152]{1,0:T(8,128)(2,1)S(1)} %shard_map.42), channel_id=1, source_target_pairs={{0,64},{32,96},{64,128},{96,288},{128,256},{160,224},{1,65},{33,97... | collective-permute-start | bytes 884744 | tf_op jit(solution)/shard_map/ppermute | solution.py:41
  18.6 30.3 %collective-permute-start.1 = (bf16[128,1152]{1,0:T(8,128)(2,1)S(1)}, bf16[128,1152]{1,0:T(8,128)(2,1)}, u32[]{:S(2)}, u32[]{:S(2)}) collective-permute-start(bf16[128,1152]{1,0:T(8,128)(2,1)S(1)} %shard_map.41), channel_id=1, source_target_pairs={{0,64},{32,288},{64,256},{96,160},{128,192},{160,224},{1,65},{33,2... | collective-permute-start | bytes 884744 | tf_op jit(solution)/shard_map/ppermute | solution.py:41
  40.7 10.4 %collective-permute-start.7 = (bf16[256,1152]{1,0:T(8,128)(2,1)S(1)}, bf16[256,1152]{1,0:T(8,128)(2,1)S(1)}, u32[]{:S(2)}, u32[]{:S(2)}) collective-permute-start(bf16[256,1152]{1,0:T(8,128)(2,1)S(1)} %get-tuple-element.8), channel_id=1, source_target_pairs={{0,32},{32,0},{64,96},{96,64},{128,160},{160,128},{192,224},{224,1... | collective-permute-start | bytes 1769480 | tf_op jit(solution)/shard_map/ppermute | solution.py:41
  52.8 40.7 %collective-permute-start.9 = (bf16[272,1152]{1,0:T(8,128)(2,1)S(1)}, bf16[272,1152]{1,0:T(8,128)(2,1)S(1)}, u32[]{:S(2)}, u32[]{:S(2)}) collective-permute-start(bf16[272,1152]{1,0:T(8,128)(2,1)S(1)} %shard_map.46.code), channel_id=1, source_target_pairs={{0,1},{1,2},{2,3},{3,4},{4,5},{5,6},{6,7},{7,8},{8,9},{9,10},{10,1... | collective-permute-start | bytes 1880072 | tf_op jit(solution)/shard_map/ppermute | solution.py:175
  63.5 12.5 %collective-permute-start.8 = (bf16[256,1152]{1,0:T(8,128)(2,1)S(1)}, bf16[256,1152]{1,0:T(8,128)(2,1)S(1)}, u32[]{:S(2)}, u32[]{:S(2)}) collective-permute-start(bf16[256,1152]{1,0:T(8,128)(2,1)S(1)} %shard_map.47), channel_id=1, source_target_pairs={{0,32},{32,0},{64,96},{96,64},{128,160},{160,128},{192,224},{224,1... | collective-permute-start | bytes 1769480 | tf_op jit(solution)/shard_map/ppermute | solution.py:41

commit v4 on v3

--- a/solution.py
+++ b/solution.py
@@ -29,7 +29,8 @@
 
 PLANES = ((0, 2), (1, 0), (2, 1))
 CORES = range(2)
-MOVE_ALL = pairs(*(((x, c), (x + 1, 0, c)) for x in range(3) for c in CORES), *(((3, c), (0, 4, c)) for c in CORES))
+MOVE_STRAIGHT = pairs(*(((3, c), (0, 4, c)) for c in CORES))
+MOVE_NEAR = pairs(*(((x, c), (x + 1, 0, c)) for x in range(3) for c in CORES))
 MOVE_OUT = [pairs(*(m for c in CORES for m in (((3, c), (p[c], 0, c)), ((p[c], c), (p[c] + 1, 0, c))))) for p in PLANES]
 MOVE_ON = [
     pairs(*(((x, c), (0, 4, c) if x == p[c] else (x + 1, 0, c)) for x in range(3) for c in CORES)) for p in PLANES
@@ -72,17 +73,27 @@
     choose(relay[0], out, own, sent)
 
 
-def pick_images(where, head, out0, far0, i0, i2, swap):
-    half = head.shape[0]
-    i2[:half] = head[...]
-    choose(where[1], out0, far0, i2.at[half:])
+def after_kernel(own, after, sent):
+    sent[...] = own[sent.shape[0] :]
+
+
+def pick_images(where, out0, far0, out1, far1, i0, i2, swap):
+    half = far0.shape[0]
+    choose(where[1], out0, far0, i2.at[:half])
+    choose(where[2], out1, far1, i2.at[half:])
     choose(where[0], i2, i0, swap)
 
 
-def part_kernel(where, out1, far1, out2, far2, i2, i0, t2, out):
-    half = far1.shape[0]
-    choose(where[2], out1, far1, t2.at[:half])
-    choose(where[3], out2, far2, t2.at[half:])
+def pick_texts(where, out2, far2, straight, picked):
+    half = far2.shape[0]
+    choose(where[3], out2, far2, picked.at[:half])
+    picked[half:] = straight[...]
+
+
+def part_kernel(where, picked, near, i2, i0, t2, out):
+    half = near.shape[0]
+    t2[:half] = picked[:half]
+    choose(where[4], picked.at[half:], near, t2.at[half:])
     text = t2[...]
     out[...] = dot_tn(coefs(i2[...], text, True), i2[...]) + dot_tn(coefs(i0[...], text, False), i0[...])
 
@@ -99,7 +110,7 @@
     code[rows:] = jnp.broadcast_to(power, (code.shape[0] - rows, acc.shape[1])).astype(jnp.bfloat16)
 
 
-def pick_texts(where, code, t2, t0, swap):
+def swap_texts(where, code, t2, t0, swap):
     choose(where[0], t2, t0, swap)
 
 
@@ -133,7 +144,7 @@
     core = blk % 2
     x = (blk // 2) % 4
     plane = [jnp.where(core == 0, *p) for p in PLANES]
-    where = jnp.stack([core] + [(x == p + 1).astype(jnp.int32) for p in plane])
+    where = jnp.stack([core] + [(x == p + 1).astype(jnp.int32) for p in plane] + [(x == 0).astype(jnp.int32)])
 
     vm = pl.BlockSpec(memory_space=pltpu.VMEM)
     sm = pl.BlockSpec(memory_space=pltpu.SMEM)
@@ -158,22 +169,22 @@
 
     full = jax.ShapeDtypeStruct((rows, width), jnp.float32)
 
-    pieces = (own_i[half:], own_t[:half], own_t[half:])
+    pieces = (own_i[:half], own_i[half:], own_t[:half])
     out = [move(p, t) for p, t in zip(pieces, MOVE_OUT)]
-    head = move(own_i[:half], MOVE_ALL)
+    straight = move(own_t[half:], MOVE_STRAIGHT)
     far = []
     for q, o, p, t in zip(plane, out, pieces, MOVE_ON):
         relay = (x == q).astype(jnp.int32).reshape(1)
         far.append(move(call(relay_kernel, bf(half), [sm] + [vm] * 2, 0)(relay, o, p), t))
-    i2, swap_i = call(pick_images, (bf(rows),) * 2, [sm] + [vm] * 4, 0)(where, head, out[0], far[0], own_i)
+    near = move(call(after_kernel, bf(half), [vm, anywhere], 0)(own_t, out[2]), MOVE_NEAR)
+    i2, swap_i = call(pick_images, (bf(rows),) * 2, [sm] + [vm] * 5, 0)(where, out[0], far[0], out[1], far[1], own_i)
     i1 = move(swap_i, MOVE_SWAP)
-    t2, part = call(part_kernel, (bf(rows), full), [sm] + [vm] * 6, 60)(
-        where, out[1], far[1], out[2], far[2], i2, own_i
-    )
+    picked = call(pick_texts, bf(rows), [sm] + [vm] * 3, 20)(where, out[2], far[2], straight)
+    t2, part = call(part_kernel, (bf(rows), full), [sm] + [vm] * 4, 60)(where, picked, near, i2, own_i)
     code = call(text_kernel, bf(rows + EXTRA), [vm] * 3, 1)(part, i1, t2)
     count = lax.axis_size("group")
     got = lax.ppermute(code, "group", [(s, (s + 1) % count) for s in range(count)])
-    t1 = move(call(pick_texts, bf(rows), [sm, anywhere] + [vm] * 2, 0)(where, code, t2, own_t), MOVE_SWAP)
+    t1 = move(call(swap_texts, bf(rows), [sm, anywhere] + [vm] * 2, 0)(where, code, t2, own_t), MOVE_SWAP)
     image_grad = call(image_kernel, full, [vm] * 4, 0)(own_i, own_t, t1, t2)
     cut = rows // 4
     text_grad = call(

time: 95.9 us -> 93.9 us (0.979)
  waiting for transfers between devices: 26.4 us -> 13.4 us
  starting transfers between devices: 55.8 us -> 65.9 us
    ppermute x9 -> x10, starting transfers between devices: 45.7 us -> 62.8 us  [move(): return lax.ppermute(value, AXES, table)]
    ppermute x1, waiting for transfers between devices: 14.7 us -> 6.73 us  [body(): lax.ppermute(code, 'group', [(s, (s + 1) % count) for s in range(count)])]
    ppermute x1, starting transfers between devices: 10.1 us -> 3.07 us  [body(): lax.ppermute(code, 'group', [(s, (s + 1) % count) for s in range(count)])]
    ppermute x9 -> x10, waiting for transfers between devices: 11.7 us -> 6.66 us  [move(): return lax.ppermute(value, AXES, table)]
    pallas_call x3 -> x5, Pallas kernels: 3.83 us -> 4.46 us  [the longest x1 1.65 us: body(): call(part_kernel, (bf(rows), full), [sm] + [vm] * 4, 60)]
  transfers between devices with their start and end apart: 10 -> 11, of which waited for: 5 -> 5; matrix products, arithmetic and copies ran while one was open for 0% -> 1% of each run, Pallas kernels for 7% -> 8%
where the time goes in v4:
time: 93.9 us; the launch traced here: 93.2 us
  starting transfers between devices  65.9 us (70%)
  waiting for transfers between devices  13.4 us (14%)
  Pallas kernels  11 us (12%)
  local copies, waits for them, and re-layouts  2.02 us (2%)
  between operations  0.94 us (1%)
    ppermute x10, starting transfers between devices, move(): return lax.ppermute(value, AXES, table)  62.8 us
    ppermute x1, waiting for transfers between devices, body(): lax.ppermute(code, 'group', [(s, (s + 1) % count) for s in range(count)])  6.73 us
    ppermute x10, waiting for transfers between devices, move(): return lax.ppermute(value, AXES, table)  6.66 us
    ppermute x1, starting transfers between devices, body(): lax.ppermute(code, 'group', [(s, (s + 1) % count) for s in range(count)])  3.07 us
    pallas_call x1, Pallas kernels, body(): image_grad = call(image_kernel, full, [vm] * 4, 0)(own_i, own_t, t1, t2)  2.75 us
    pallas_call x1, Pallas kernels, body(): call(read_kernel, full, [vm], 0, out_specs=pl.BlockSpec((cut, width), lam...  2.03 us
  transfers between devices with their start and end apart: 11, of which 5 were waited for; matrix products, arithmetic and copies ran while one was open for 1% of the time, Pallas kernels for 8%

profile of v4, /device:TPU:1, one launch (start us, length us, event | category | flops | bytes accessed | tf_op | source)
XLA Modules:
  0.0 93.2 jit_solution(12440211633771997452)
XLA Ops:
  0.6 1.2 %slice_bitcast_fusion = (bf16[128,1152]{1,0:T(8,128)(2,1)S(1)}, bf16[128,1152]{1,0:T(8,128)(2,1)S(1)}) fusion(bf16[1,1,256,1152]{3,2,1,0:T(8,128)(2,1)} %param.2), kind=kLoop, calls=%fused_computation | loop fusion | bytes 1179648 | tf_op jit(solution)/shard_map/slice | solution.py:172
  1.8 3.9 %collective-permute-start.6 = (bf16[128,1152]{1,0:T(8,128)(2,1)S(1)}, bf16[128,1152]{1,0:T(8,128)(2,1)S(1)}, u32[]{:S(2)}, u32[]{:S(2)}) collective-permute-start(bf16[128,1152]{1,0:T(8,128)(2,1)S(1)} %get-tuple-element.10.own), channel_id=1, source_target_pairs={{192,64},{64,128},{224,32},{32,96},{193,65},{65,129},{225,33},{33,... | collective-permute-start | bytes 884744 | tf_op jit(solution)/shard_map/ppermute | solution.py:42
  5.8 0.7 collective-permute-start.4
  6.5 0.8 slice_bitcast_fusion.2
  7.2 0.7 collective-permute-start
  7.9 1.3 %collective-permute-start.2 = (bf16[128,1152]{1,0:T(8,128)(2,1)}, bf16[128,1152]{1,0:T(8,128)(2,1)}, u32[]{:S(2)}, u32[]{:S(2)}) collective-permute-start(bf16[128,1152]{1,0:T(8,128)(2,1)} %get-tuple-element.12), channel_id=1, source_target_pairs={{192,256},{224,288},{193,257},{225,289},{194,258},{226,290},{195,2... | collective-permute-start | bytes 884744 | tf_op jit(solution)/shard_map/ppermute | solution.py:42
  9.2 1.3 %collective-permute-done.6.out.out1 = bf16[128,1152]{1,0:T(8,128)(2,1)S(1)} collective-permute-done((bf16[128,1152]{1,0:T(8,128)(2,1)S(1)}, bf16[128,1152]{1,0:T(8,128)(2,1)S(1)}, u32[]{:S(2)}, u32[]{:S(2)}) %collective-permute-start.6) | collective-permute-done | bytes 294944 | tf_op jit(solution)/shard_map/ppermute | solution.py:42
  10.5 11.4 %collective-permute-start.7 = (bf16[128,1152]{1,0:T(8,128)(2,1)S(1)}, bf16[128,1152]{1,0:T(8,128)(2,1)S(1)}, u32[]{:S(2)}, u32[]{:S(2)}) collective-permute-start(bf16[128,1152]{1,0:T(8,128)(2,1)S(1)} %shard_map.45), channel_id=1, source_target_pairs={{0,64},{32,288},{64,256},{96,160},{128,192},{160,224},{1,65},{33,2... | collective-permute-start | bytes 884744 | tf_op jit(solution)/shard_map/ppermute | solution.py:42
  22.0 2.1 %collective-permute-start.5 = (bf16[128,1152]{1,0:T(8,128)(2,1)S(1)}, bf16[128,1152]{1,0:T(8,128)(2,1)}, u32[]{:S(2)}, u32[]{:S(2)}) collective-permute-start(bf16[128,1152]{1,0:T(8,128)(2,1)S(1)} %shard_map.44), channel_id=1, source_target_pairs={{0,256},{32,96},{64,128},{96,160},{128,192},{160,288},{1,257},{33,... | collective-permute-start | bytes 884744 | tf_op jit(solution)/shard_map/ppermute | solution.py:42
  24.2 4.4 %collective-permute-start.1 = (bf16[128,1152]{1,0:T(8,128)(2,1)S(1)}, bf16[128,1152]{1,0:T(8,128)(2,1)}, u32[]{:S(2)}, u32[]{:S(2)}) collective-permute-start(bf16[128,1152]{1,0:T(8,128)(2,1)S(1)} %shard_map.41), channel_id=1, source_target_pairs={{0,64},{32,96},{64,128},{96,288},{128,256},{160,224},{1,65},{33,97... | collective-permute-start | bytes 884744 | tf_op jit(solution)/shard_map/ppermute | solution.py:42
  28.7 9.4 %collective-permute-start.3 = (bf16[128,1152]{1,0:T(8,128)(2,1)S(1)}, bf16[128,1152]{1,0:T(8,128)(2,1)S(1)}, u32[]{:S(2)}, u32[]{:S(2)}) collective-permute-start(bf16[128,1152]{1,0:T(8,128)(2,1)S(1)} %shard_map.43), channel_id=1, source_target_pairs={{0,64},{32,96},{64,128},{96,160},{128,192},{160,224},{1,65},{33,97... | collective-permute-start | bytes 884744 | tf_op jit(solution)/shard_map/ppermute | solution.py:42
  38.1 2.1 %collective-permute-done.5.far0 = bf16[128,1152]{1,0:T(8,128)(2,1)} collective-permute-done((bf16[128,1152]{1,0:T(8,128)(2,1)S(1)}, bf16[128,1152]{1,0:T(8,128)(2,1)}, u32[]{:S(2)}, u32[]{:S(2)}) %collective-permute-start.5) | collective-permute-done | bytes 294944 | tf_op jit(solution)/shard_map/ppermute | solution.py:42
  40.1 1.1 %shard_map.46 = (bf16[256,1152]{1,0:T(8,128)(2,1)S(1)}, bf16[256,1152]{1,0:T(8,128)(2,1)S(1)}) custom-call(s32[5]{0:T(128)S(1)} %stack.39.where, bf16[128,1152]{1,0:T(8,128)(2,1)S(1)} %collective-permute-done.4.out.out0, bf16[128,1152]{1,0:T(8,128)(2,1)} %collective-permute-done.5.far0, bf16[128,1152]{1,0:T(8,128)(2,1)S(1)} %collective-permute-done.6.out.out1, ...), custom_call_target="tpu_custom_call" | custom-call | bytes 2097152 | tf_op jit(solution)/shard_map/pallas_call | solution.py:180
  41.2 19.1 %collective-permute-start.8 = (bf16[256,1152]{1,0:T(8,128)(2,1)S(1)}, bf16[256,1152]{1,0:T(8,128)(2,1)S(1)}, u32[]{:S(2)}, u32[]{:S(2)}) collective-permute-start(bf16[256,1152]{1,0:T(8,128)(2,1)S(1)} %get-tuple-element.8), channel_id=1, source_target_pairs={{0,32},{32,0},{64,96},{96,64},{128,160},{160,128},{192,224},{224,1... | collective-permute-start | bytes 1769480 | tf_op jit(solution)/shard_map/ppermute | solution.py:42
  60.3 1.7 %collective-permute-done.1.far2 = bf16[128,1152]{1,0:T(8,128)(2,1)} collective-permute-done((bf16[128,1152]{1,0:T(8,128)(2,1)S(1)}, bf16[128,1152]{1,0:T(8,128)(2,1)}, u32[]{:S(2)}, u32[]{:S(2)}) %collective-permute-start.1) | collective-permute-done | bytes 294944 | tf_op jit(solution)/shard_map/ppermute | solution.py:42
  62.1 1.1 %shard_map.42.picked = bf16[256,1152]{1,0:T(8,128)(2,1)S(1)} custom-call(s32[5]{0:T(128)S(1)} %stack.39.where, bf16[128,1152]{1,0:T(8,128)(2,1)S(1)} %collective-permute-done.out.out2.after, bf16[128,1152]{1,0:T(8,128)(2,1)} %collective-permute-done.1.far2, bf16[128,1152]{1,0:T(8,128)(2,1)} %collective-permute-done.2.straight), custom_call_target="tpu_custom_call" | custom-call | flops 6039797760 | bytes 2097152 | tf_op jit(solution)/shard_map/pallas_call | solution.py:182
  63.2 1.7 %shard_map.47 = (bf16[256,1152]{1,0:T(8,128)(2,1)S(1)}, f32[256,1152]{1,0:T(8,128)S(1)}) custom-call(s32[5]{0:T(128)S(1)} %stack.39.where, bf16[256,1152]{1,0:T(8,128)(2,1)S(1)} %shard_map.42.picked, bf16[128,1152]{1,0:T(8,128)(2,1)S(1)} %collective-permute-done.3.near, bf16[256,1152]{1,0:T(8,128)(2,1)S(1)} %get-tuple-element.6.i2, ...), custom_call_target="tpu_custom_call" | custom-call | flops 18119393280 | bytes 2097152 | tf_op jit(solution)/shard_map/pallas_call | solution.py:183
  64.9 1.7 %shard_map.48.code = bf16[272,1152]{1,0:T(8,128)(2,1)S(1)} custom-call(f32[256,1152]{1,0:T(8,128)S(1)} %get-tuple-element.7.part, bf16[256,1152]{1,0:T(8,128)(2,1)S(1)} %collective-permute-done.8.i1, bf16[256,1152]{1,0:T(8,128)(2,1)S(1)} %get-tuple-element.9.t2), custom_call_target="tpu_custom_call" | custom-call | flops 301989888 | bytes 2097152 | tf_op jit(solution)/shard_map/pallas_call | solution.py:184
  66.5 3.1 %collective-permute-start.10 = (bf16[272,1152]{1,0:T(8,128)(2,1)S(1)}, bf16[272,1152]{1,0:T(8,128)(2,1)S(1)}, u32[]{:S(2)}, u32[]{:S(2)}) collective-permute-start(bf16[272,1152]{1,0:T(8,128)(2,1)S(1)} %shard_map.48.code), channel_id=1, source_target_pairs={{0,1},{1,2},{2,3},{3,4},{4,5},{5,6},{6,7},{7,8},{8,9},{9,10},{10,1... | collective-permute-start | bytes 1880072 | tf_op jit(solution)/shard_map/ppermute | solution.py:186
  70.2 9.9 %collective-permute-start.9 = (bf16[256,1152]{1,0:T(8,128)(2,1)S(1)}, bf16[256,1152]{1,0:T(8,128)(2,1)S(1)}, u32[]{:S(2)}, u32[]{:S(2)}) collective-permute-start(bf16[256,1152]{1,0:T(8,128)(2,1)S(1)} %shard_map.49), channel_id=1, source_target_pairs={{0,32},{32,0},{64,96},{96,64},{128,160},{160,128},{192,224},{224,1... | collective-permute-start | bytes 1769480 | tf_op jit(solution)/shard_map/ppermute | solution.py:42
  80.1 1.6 %collective-permute-done.9.t1 = bf16[256,1152]{1,0:T(8,128)(2,1)S(1)} collective-permute-done((bf16[256,1152]{1,0:T(8,128)(2,1)S(1)}, bf16[256,1152]{1,0:T(8,128)(2,1)S(1)}, u32[]{:S(2)}, u32[]{:S(2)}) %collective-permute-start.9) | collective-permute-done | bytes 589856 | tf_op jit(solution)/shard_map/ppermute | solution.py:42
  81.7 2.7 %shard_map.50 = f32[256,1152]{1,0:T(8,128)} custom-call(bf16[256,1152]{1,0:T(8,128)(2,1)S(1)} %bitcast.25, bf16[256,1152]{1,0:T(8,128)(2,1)S(1)} %bitcast.22, bf16[256,1152]{1,0:T(8,128)(2,1)S(1)} %collective-permute-done.9.t1, bf16[256,1152]{1,0:T(8,128)(2,1)S(1)} %get-tuple-element.9.t2), custom_call_target="tpu_custom_call" | custom-call | bytes 2097152 | tf_op jit(solution)/shard_map/pallas_call | solution.py:188
  84.4 6.7 %collective-permute-done.10.code = bf16[272,1152]{1,0:T(8,128)(2,1)S(1)} collective-permute-done((bf16[272,1152]{1,0:T(8,128)(2,1)S(1)}, bf16[272,1152]{1,0:T(8,128)(2,1)S(1)}, u32[]{:S(2)}, u32[]{:S(2)}) %collective-permute-start.10) | collective-permute-done | bytes 626720 | tf_op jit(solution)/shard_map/ppermute | solution.py:186
  91.2 2.0 %shard_map.51 = f32[256,1152]{1,0:T(8,128)} custom-call(bf16[272,1152]{1,0:T(8,128)(2,1)S(1)} %collective-permute-done.10.code), custom_call_target="tpu_custom_call" | custom-call | bytes 2097152 | tf_op jit(solution)/shard_map/pallas_call | solution.py:190
  (16 shorter events, 0.8 us)
Async XLA Ops:
  0.6 5.8 %copy-start = (bf16[1,1,256,1152]{3,2,1,0:T(8,128)(2,1)S(1)}, bf16[1,1,256,1152]{3,2,1,0:T(8,128)(2,1)}, u32[]{:S(2)}) copy-start(bf16[1,1,256,1152]{3,2,1,0:T(8,128)(2,1)} %param.3) | copy-start | bytes 1769476
  1.8 8.7 %collective-permute-start.6 = (bf16[128,1152]{1,0:T(8,128)(2,1)S(1)}, bf16[128,1152]{1,0:T(8,128)(2,1)S(1)}, u32[]{:S(2)}, u32[]{:S(2)}) collective-permute-start(bf16[128,1152]{1,0:T(8,128)(2,1)S(1)} %get-tuple-element.10.own), channel_id=1, source_target_pairs={{192,64},{64,128},{224,32},{32,96},{193,65},{65,129},{225,33},{33,... | collective-permute-start | bytes 884744 | tf_op jit(solution)/shard_map/ppermute | solution.py:42
  5.8 16.2 %collective-permute-start.4 = (bf16[128,1152]{1,0:T(8,128)(2,1)S(1)}, bf16[128,1152]{1,0:T(8,128)(2,1)S(1)}, u32[]{:S(2)}, u32[]{:S(2)}) collective-permute-start(bf16[128,1152]{1,0:T(8,128)(2,1)S(1)} %get-tuple-element.11.own), channel_id=1, source_target_pairs={{192,0},{0,64},{224,160},{160,224},{193,1},{1,65},{225,161},{161,2... | collective-permute-start | bytes 884744 | tf_op jit(solution)/shard_map/ppermute | solution.py:42
  7.2 16.9 %collective-permute-start = (bf16[128,1152]{1,0:T(8,128)(2,1)S(1)}, bf16[128,1152]{1,0:T(8,128)(2,1)S(1)}, u32[]{:S(2)}, u32[]{:S(2)}) collective-permute-start(bf16[128,1152]{1,0:T(8,128)(2,1)S(1)} %get-tuple-element.13.own), channel_id=1, source_target_pairs={{192,128},{128,192},{224,96},{96,160},{193,129},{129,193},{225,97}... | collective-permute-start | bytes 884744 | tf_op jit(solution)/shard_map/ppermute | solution.py:42
  7.9 52.4 %collective-permute-start.2 = (bf16[128,1152]{1,0:T(8,128)(2,1)}, bf16[128,1152]{1,0:T(8,128)(2,1)}, u32[]{:S(2)}, u32[]{:S(2)}) collective-permute-start(bf16[128,1152]{1,0:T(8,128)(2,1)} %get-tuple-element.12), channel_id=1, source_target_pairs={{192,256},{224,288},{193,257},{225,289},{194,258},{226,290},{195,2... | collective-permute-start | bytes 884744 | tf_op jit(solution)/shard_map/ppermute | solution.py:42
  10.5 27.5 %collective-permute-start.7 = (bf16[128,1152]{1,0:T(8,128)(2,1)S(1)}, bf16[128,1152]{1,0:T(8,128)(2,1)S(1)}, u32[]{:S(2)}, u32[]{:S(2)}) collective-permute-start(bf16[128,1152]{1,0:T(8,128)(2,1)S(1)} %shard_map.45), channel_id=1, source_target_pairs={{0,64},{32,288},{64,256},{96,160},{128,192},{160,224},{1,65},{33,2... | collective-permute-start | bytes 884744 | tf_op jit(solution)/shard_map/ppermute | solution.py:42
  22.0 18.1 %copy-start.1 = (bf16[1,1,256,1152]{3,2,1,0:T(8,128)(2,1)S(1)}, bf16[1,1,256,1152]{3,2,1,0:T(8,128)(2,1)}, u32[]{:S(2)}) copy-start(bf16[1,1,256,1152]{3,2,1,0:T(8,128)(2,1)} %param.2) | copy-start | bytes 1769476
  22.0 18.1 %collective-permute-start.5 = (bf16[128,1152]{1,0:T(8,128)(2,1)S(1)}, bf16[128,1152]{1,0:T(8,128)(2,1)}, u32[]{:S(2)}, u32[]{:S(2)}) collective-permute-start(bf16[128,1152]{1,0:T(8,128)(2,1)S(1)} %shard_map.44), channel_id=1, source_target_pairs={{0,256},{32,96},{64,128},{96,160},{128,192},{160,288},{1,257},{33,... | collective-permute-start | bytes 884744 | tf_op jit(solution)/shard_map/ppermute | solution.py:42
  24.2 37.9 %collective-permute-start.1 = (bf16[128,1152]{1,0:T(8,128)(2,1)S(1)}, bf16[128,1152]{1,0:T(8,128)(2,1)}, u32[]{:S(2)}, u32[]{:S(2)}) collective-permute-start(bf16[128,1152]{1,0:T(8,128)(2,1)S(1)} %shard_map.41), channel_id=1, source_target_pairs={{0,64},{32,96},{64,128},{96,288},{128,256},{160,224},{1,65},{33,97... | collective-permute-start | bytes 884744 | tf_op jit(solution)/shard_map/ppermute | solution.py:42
  28.7 34.5 %collective-permute-start.3 = (bf16[128,1152]{1,0:T(8,128)(2,1)S(1)}, bf16[128,1152]{1,0:T(8,128)(2,1)S(1)}, u32[]{:S(2)}, u32[]{:S(2)}) collective-permute-start(bf16[128,1152]{1,0:T(8,128)(2,1)S(1)} %shard_map.43), channel_id=1, source_target_pairs={{0,64},{32,96},{64,128},{96,160},{128,192},{160,224},{1,65},{33,97... | collective-permute-start | bytes 884744 | tf_op jit(solution)/shard_map/ppermute | solution.py:42
  41.2 23.6 %collective-permute-start.8 = (bf16[256,1152]{1,0:T(8,128)(2,1)S(1)}, bf16[256,1152]{1,0:T(8,128)(2,1)S(1)}, u32[]{:S(2)}, u32[]{:S(2)}) collective-permute-start(bf16[256,1152]{1,0:T(8,128)(2,1)S(1)} %get-tuple-element.8), channel_id=1, source_target_pairs={{0,32},{32,0},{64,96},{96,64},{128,160},{160,128},{192,224},{224,1... | collective-permute-start | bytes 1769480 | tf_op jit(solution)/shard_map/ppermute | solution.py:42
  66.5 24.6 %collective-permute-start.10 = (bf16[272,1152]{1,0:T(8,128)(2,1)S(1)}, bf16[272,1152]{1,0:T(8,128)(2,1)S(1)}, u32[]{:S(2)}, u32[]{:S(2)}) collective-permute-start(bf16[272,1152]{1,0:T(8,128)(2,1)S(1)} %shard_map.48.code), channel_id=1, source_target_pairs={{0,1},{1,2},{2,3},{3,4},{4,5},{5,6},{6,7},{7,8},{8,9},{9,10},{10,1... | collective-permute-start | bytes 1880072 | tf_op jit(solution)/shard_map/ppermute | solution.py:186
  70.2 11.5 %collective-permute-start.9 = (bf16[256,1152]{1,0:T(8,128)(2,1)S(1)}, bf16[256,1152]{1,0:T(8,128)(2,1)S(1)}, u32[]{:S(2)}, u32[]{:S(2)}) collective-permute-start(bf16[256,1152]{1,0:T(8,128)(2,1)S(1)} %shard_map.49), channel_id=1, source_target_pairs={{0,32},{32,0},{64,96},{96,64},{128,160},{160,128},{192,224},{224,1... | collective-permute-start | bytes 1769480 | tf_op jit(solution)/shard_map/ppermute | solution.py:42

commit v5 on v3

--- a/solution.py
+++ b/solution.py
@@ -29,11 +29,10 @@
 
 PLANES = ((0, 2), (1, 0), (2, 1))
 CORES = range(2)
-MOVE_ALL = pairs(*(((x, c), (x + 1, 0, c)) for x in range(3) for c in CORES), *(((3, c), (0, 4, c)) for c in CORES))
-MOVE_OUT = [pairs(*(m for c in CORES for m in (((3, c), (p[c], 0, c)), ((p[c], c), (p[c] + 1, 0, c))))) for p in PLANES]
-MOVE_ON = [
-    pairs(*(((x, c), (0, 4, c) if x == p[c] else (x + 1, 0, c)) for x in range(3) for c in CORES)) for p in PLANES
-]
+MOVE_STRAIGHT = pairs(*(((3, c), (0, 4, c)) for c in CORES))
+MOVE_NEAR = pairs(*(((x, c), (x + 1, 0, c)) for x in range(3) for c in CORES))
+MOVE_OUT = [pairs(*(((3, c), (p[c], 0, c)) for c in CORES)) for p in PLANES]
+MOVE_ON = [pairs(*(((p[c], c), (0, 4, c)) for c in CORES)) for p in PLANES]
 MOVE_SWAP = pairs(*(((x, c), (x, 0, 1 - c)) for x in range(4) for c in CORES))
 
 
@@ -68,21 +67,34 @@
         out[...] = b[...]
 
 
-def relay_kernel(relay, out, own, sent):
-    choose(relay[0], out, own, sent)
+def near_kernel(images, texts, both, sems):
+    rows = images.shape[0]
+    copies = [
+        pltpu.make_async_copy(images, both.at[pl.ds(0, rows)], sems.at[0]),
+        pltpu.make_async_copy(texts, both.at[pl.ds(rows, rows)], sems.at[1]),
+    ]
+    for copy in copies:
+        copy.start()
+    for copy in copies:
+        copy.wait()
 
 
-def pick_images(where, head, out0, far0, i0, i2, swap):
-    half = head.shape[0]
-    i2[:half] = head[...]
-    choose(where[1], out0, far0, i2.at[half:])
+def far_kernel(far0, far1, far2, straight, images):
+    half = far0.shape[0]
+    images[:half] = far0[...]
+    images[half:] = far1[...]
+
+
+def pick_images(where, far, near, i0, i2, swap):
+    rows = i0.shape[0]
+    choose(where[1], far, near.at[:rows], i2)
     choose(where[0], i2, i0, swap)
 
 
-def part_kernel(where, out1, far1, out2, far2, i2, i0, t2, out):
-    half = far1.shape[0]
-    choose(where[2], out1, far1, t2.at[:half])
-    choose(where[3], out2, far2, t2.at[half:])
+def part_kernel(where, far2, straight, near, i2, i0, t2, out):
+    half = far2.shape[0]
+    choose(where[1], far2, near.at[2 * half : 3 * half], t2.at[:half])
+    choose(where[1], straight, near.at[3 * half :], t2.at[half:])
     text = t2[...]
     out[...] = dot_tn(coefs(i2[...], text, True), i2[...]) + dot_tn(coefs(i0[...], text, False), i0[...])
 
@@ -132,8 +144,7 @@
     blk = lax.axis_index("blk")
     core = blk % 2
     x = (blk // 2) % 4
-    plane = [jnp.where(core == 0, *p) for p in PLANES]
-    where = jnp.stack([core] + [(x == p + 1).astype(jnp.int32) for p in plane])
+    where = jnp.stack([core, (x == 0).astype(jnp.int32)])
 
     vm = pl.BlockSpec(memory_space=pltpu.VMEM)
     sm = pl.BlockSpec(memory_space=pltpu.SMEM)
@@ -158,18 +169,16 @@
 
     full = jax.ShapeDtypeStruct((rows, width), jnp.float32)
 
-    pieces = (own_i[half:], own_t[:half], own_t[half:])
+    pieces = (own_i[:half], own_i[half:], own_t[:half])
     out = [move(p, t) for p, t in zip(pieces, MOVE_OUT)]
-    head = move(own_i[:half], MOVE_ALL)
-    far = []
-    for q, o, p, t in zip(plane, out, pieces, MOVE_ON):
-        relay = (x == q).astype(jnp.int32).reshape(1)
-        far.append(move(call(relay_kernel, bf(half), [sm] + [vm] * 2, 0)(relay, o, p), t))
-    i2, swap_i = call(pick_images, (bf(rows),) * 2, [sm] + [vm] * 4, 0)(where, head, out[0], far[0], own_i)
+    straight = move(own_t[half:], MOVE_STRAIGHT)
+    far = [move(o, t) for o, t in zip(out, MOVE_ON)]
+    both = call(near_kernel, bf(2 * rows), [anywhere] * 2, 0, scratch=[pltpu.SemaphoreType.DMA((2,))])(own_i, own_t)
+    near = move(both, MOVE_NEAR)
+    beyond = call(far_kernel, bf(rows), [vm, vm, anywhere, anywhere], 36)(*far, straight)
+    i2, swap_i = call(pick_images, (bf(rows),) * 2, [sm] + [vm] * 3, 0)(where, beyond, near, own_i)
     i1 = move(swap_i, MOVE_SWAP)
-    t2, part = call(part_kernel, (bf(rows), full), [sm] + [vm] * 6, 60)(
-        where, out[1], far[1], out[2], far[2], i2, own_i
-    )
+    t2, part = call(part_kernel, (bf(rows), full), [sm] + [vm] * 5, 2)(where, far[2], straight, near, i2, own_i)
     code = call(text_kernel, bf(rows + EXTRA), [vm] * 3, 1)(part, i1, t2)
     count = lax.axis_size("group")
     got = lax.ppermute(code, "group", [(s, (s + 1) % count) for s in range(count)])

time: 95.9 us -> 101 us (1.053)
  the two profiles are of different devices: /device:TPU:1 before, /device:TPU:7 now
where the time goes in v5:
time: 101 us
  waiting for transfers between devices  52.5 us (52%)
  starting transfers between devices  34 us (34%)
  Pallas kernels  11.2 us (11%)
  local copies, waits for them, and re-layouts  1.96 us (2%)
    ppermute x10, waiting for transfers between devices, move(): return lax.ppermute(value, AXES, table)  39.4 us
    ppermute x10, starting transfers between devices, move(): return lax.ppermute(value, AXES, table)  29.1 us
    ppermute x1, waiting for transfers between devices, body(): lax.ppermute(code, 'group', [(s, (s + 1) % count) for s in range(count)])  13.1 us
    ppermute x1, starting transfers between devices, body(): lax.ppermute(code, 'group', [(s, (s + 1) % count) for s in range(count)])  4.96 us
    pallas_call x1, Pallas kernels, body(): image_grad = call(image_kernel, full, [vm] * 4, 0)(own_i, own_t, t1, t2)  2.76 us
    pallas_call x1, Pallas kernels, body(): call(part_kernel, (bf(rows), full), [sm] + [vm] * 5, 2)  2.18 us
    pallas_call x1, Pallas kernels, body(): call(read_kernel, full, [vm], 0, out_specs=pl.BlockSpec((cut, width), lam...  2.03 us
  transfers between devices with their start and end apart: 11, of which 3 were waited for; matrix products, arithmetic and copies ran while one was open for 1% of the time, Pallas kernels for 7%

profile of v5, /device:TPU:7, one launch (start us, length us, event | category | flops | bytes accessed | tf_op | source)
XLA Modules:
  0.0 100.6 jit_solution(2715025606482650578)
XLA Ops:
  0.6 1.2 %slice_bitcast_fusion = (bf16[128,1152]{1,0:T(8,128)(2,1)S(1)}, bf16[128,1152]{1,0:T(8,128)(2,1)S(1)}) fusion(bf16[1,1,256,1152]{3,2,1,0:T(8,128)(2,1)} %param.2), kind=kLoop, calls=%fused_computation | loop fusion | bytes 1179648 | tf_op jit(solution)/shard_map/slice | solution.py:172
  1.8 2.0 %collective-permute-start.6 = (bf16[128,1152]{1,0:T(8,128)(2,1)S(1)}, bf16[128,1152]{1,0:T(8,128)(2,1)}, u32[]{:S(2)}, u32[]{:S(2)}) collective-permute-start(bf16[128,1152]{1,0:T(8,128)(2,1)S(1)} %get-tuple-element.10), channel_id=1, source_target_pairs={{192,64},{224,32},{193,65},{225,33},{194,66},{226,34},{195,67},{22... | collective-permute-start | bytes 884744 | tf_op jit(solution)/shard_map/ppermute | solution.py:40
  3.9 2.5 %collective-permute-start.4 = (bf16[128,1152]{1,0:T(8,128)(2,1)S(1)}, bf16[128,1152]{1,0:T(8,128)(2,1)}, u32[]{:S(2)}, u32[]{:S(2)}) collective-permute-start(bf16[128,1152]{1,0:T(8,128)(2,1)S(1)} %get-tuple-element.11), channel_id=1, source_target_pairs={{192,0},{224,160},{193,1},{225,161},{194,2},{226,162},{195,3},{227... | collective-permute-start | bytes 884744 | tf_op jit(solution)/shard_map/ppermute | solution.py:40
  6.4 0.8 slice_bitcast_fusion.2
  7.2 2.0 %collective-permute-start = (bf16[128,1152]{1,0:T(8,128)(2,1)S(1)}, bf16[128,1152]{1,0:T(8,128)(2,1)}, u32[]{:S(2)}, u32[]{:S(2)}) collective-permute-start(bf16[128,1152]{1,0:T(8,128)(2,1)S(1)} %get-tuple-element.13), channel_id=1, source_target_pairs={{192,128},{224,96},{193,129},{225,97},{194,130},{226,98},{195,131}... | collective-permute-start | bytes 884744 | tf_op jit(solution)/shard_map/ppermute | solution.py:40
  9.2 8.8 %collective-permute-start.2 = (bf16[128,1152]{1,0:T(8,128)(2,1)}, bf16[128,1152]{1,0:T(8,128)(2,1)}, u32[]{:S(2)}, u32[]{:S(2)}) collective-permute-start(bf16[128,1152]{1,0:T(8,128)(2,1)} %get-tuple-element.12), channel_id=1, source_target_pairs={{192,256},{224,288},{193,257},{225,289},{194,258},{226,290},{195,2... | collective-permute-start | bytes 884744 | tf_op jit(solution)/shard_map/ppermute | solution.py:40
  17.9 1.4 %collective-permute-start.7 = (bf16[128,1152]{1,0:T(8,128)(2,1)}, bf16[128,1152]{1,0:T(8,128)(2,1)}, u32[]{:S(2)}, u32[]{:S(2)}) collective-permute-start(bf16[128,1152]{1,0:T(8,128)(2,1)} %collective-permute-done.6), channel_id=1, source_target_pairs={{64,256},{32,288},{65,257},{33,289},{66,258},{34,290},{67,259},{35... | collective-permute-start | bytes 884744 | tf_op jit(solution)/shard_map/ppermute | solution.py:40
  19.3 1.4 %collective-permute-start.5 = (bf16[128,1152]{1,0:T(8,128)(2,1)}, bf16[128,1152]{1,0:T(8,128)(2,1)}, u32[]{:S(2)}, u32[]{:S(2)}) collective-permute-start(bf16[128,1152]{1,0:T(8,128)(2,1)} %collective-permute-done.4), channel_id=1, source_target_pairs={{0,256},{160,288},{1,257},{161,289},{2,258},{162,290},{3,259},{163... | collective-permute-start | bytes 884744 | tf_op jit(solution)/shard_map/ppermute | solution.py:40
  20.7 1.4 %collective-permute-start.1 = (bf16[128,1152]{1,0:T(8,128)(2,1)}, bf16[128,1152]{1,0:T(8,128)(2,1)}, u32[]{:S(2)}, u32[]{:S(2)}) collective-permute-start(bf16[128,1152]{1,0:T(8,128)(2,1)} %collective-permute-done), channel_id=1, source_target_pairs={{128,256},{96,288},{129,257},{97,289},{130,258},{98,290},{131,259}... | collective-permute-start | bytes 884744 | tf_op jit(solution)/shard_map/ppermute | solution.py:40
  22.1 0.3 shard_map.41
  22.3 1.3 %collective-permute-start.3 = (bf16[512,1152]{1,0:T(8,128)(2,1)S(1)}, bf16[512,1152]{1,0:T(8,128)(2,1)S(1)}, u32[]{:S(2)}, u32[]{:S(2)}) collective-permute-start(bf16[512,1152]{1,0:T(8,128)(2,1)S(1)} %shard_map.41), channel_id=1, source_target_pairs={{0,64},{32,96},{64,128},{96,160},{128,192},{160,224},{1,65},{33,97... | collective-permute-start | bytes 3538952 | tf_op jit(solution)/shard_map/ppermute | solution.py:40
  23.8 1.1 %shard_map.42.far = bf16[256,1152]{1,0:T(8,128)(2,1)S(1)} custom-call(bf16[128,1152]{1,0:T(8,128)(2,1)} %collective-permute-done.5.far0, bf16[128,1152]{1,0:T(8,128)(2,1)} %collective-permute-done.7.far1, bf16[128,1152]{1,0:T(8,128)(2,1)} %collective-permute-done.1.far2, bf16[128,1152]{1,0:T(8,128)(2,1)} %collective-permute-done.2.straight), custom_call_target="tpu_custom_call" | custom-call | flops 10871635968 | bytes 2097152 | tf_op jit(solution)/shard_map/pallas_call | solution.py:178
  24.9 37.7 %collective-permute-done.3.near = bf16[512,1152]{1,0:T(8,128)(2,1)S(1)} collective-permute-done((bf16[512,1152]{1,0:T(8,128)(2,1)S(1)}, bf16[512,1152]{1,0:T(8,128)(2,1)S(1)}, u32[]{:S(2)}, u32[]{:S(2)}) %collective-permute-start.3) | collective-permute-done | bytes 1179680 | tf_op jit(solution)/shard_map/ppermute | solution.py:40
  62.5 0.6 shard_map.43
  63.2 6.1 %collective-permute-start.8 = (bf16[256,1152]{1,0:T(8,128)(2,1)S(1)}, bf16[256,1152]{1,0:T(8,128)(2,1)S(1)}, u32[]{:S(2)}, u32[]{:S(2)}) collective-permute-start(bf16[256,1152]{1,0:T(8,128)(2,1)S(1)} %get-tuple-element.8), channel_id=1, source_target_pairs={{0,32},{32,0},{64,96},{96,64},{128,160},{160,128},{192,224},{224,1... | collective-permute-start | bytes 1769480 | tf_op jit(solution)/shard_map/ppermute | solution.py:40
  69.3 2.2 %shard_map.44 = (bf16[256,1152]{1,0:T(8,128)(2,1)S(1)}, f32[256,1152]{1,0:T(8,128)S(1)}) custom-call(s32[2]{0:T(128)S(1)} %pad_add_fusion.where, bf16[128,1152]{1,0:T(8,128)(2,1)} %collective-permute-done.1.far2, bf16[128,1152]{1,0:T(8,128)(2,1)} %collective-permute-done.2.straight, bf16[512,1152]{1,0:T(8,128)(2,1)S(1)} %collective-permute-done.3.near, ...), custom_call_target="tpu_custom_call" | custom-call | flops 603979776 | bytes 2097152 | tf_op jit(solution)/shard_map/pallas_call | solution.py:181
  71.5 1.7 %shard_map.45.code = bf16[272,1152]{1,0:T(8,128)(2,1)S(1)} custom-call(f32[256,1152]{1,0:T(8,128)S(1)} %get-tuple-element.7.part, bf16[256,1152]{1,0:T(8,128)(2,1)S(1)} %collective-permute-done.8.i1, bf16[256,1152]{1,0:T(8,128)(2,1)S(1)} %get-tuple-element.9.t2), custom_call_target="tpu_custom_call" | custom-call | flops 301989888 | bytes 2097152 | tf_op jit(solution)/shard_map/pallas_call | solution.py:182
  73.2 5.0 %collective-permute-start.10 = (bf16[272,1152]{1,0:T(8,128)(2,1)S(1)}, bf16[272,1152]{1,0:T(8,128)(2,1)S(1)}, u32[]{:S(2)}, u32[]{:S(2)}) collective-permute-start(bf16[272,1152]{1,0:T(8,128)(2,1)S(1)} %shard_map.45.code), channel_id=1, source_target_pairs={{0,1},{1,2},{2,3},{3,4},{4,5},{5,6},{6,7},{7,8},{8,9},{9,10},{10,1... | collective-permute-start | bytes 1880072 | tf_op jit(solution)/shard_map/ppermute | solution.py:184
  78.1 0.6 shard_map.46
  78.7 2.2 %collective-permute-start.9 = (bf16[256,1152]{1,0:T(8,128)(2,1)S(1)}, bf16[256,1152]{1,0:T(8,128)(2,1)S(1)}, u32[]{:S(2)}, u32[]{:S(2)}) collective-permute-start(bf16[256,1152]{1,0:T(8,128)(2,1)S(1)} %shard_map.46), channel_id=1, source_target_pairs={{0,32},{32,0},{64,96},{96,64},{128,160},{160,128},{192,224},{224,1... | collective-permute-start | bytes 1769480 | tf_op jit(solution)/shard_map/ppermute | solution.py:40
  81.0 1.7 %collective-permute-done.9.t1 = bf16[256,1152]{1,0:T(8,128)(2,1)S(1)} collective-permute-done((bf16[256,1152]{1,0:T(8,128)(2,1)S(1)}, bf16[256,1152]{1,0:T(8,128)(2,1)S(1)}, u32[]{:S(2)}, u32[]{:S(2)}) %collective-permute-start.9) | collective-permute-done | bytes 589856 | tf_op jit(solution)/shard_map/ppermute | solution.py:40
  82.6 2.8 %shard_map.47 = f32[256,1152]{1,0:T(8,128)} custom-call(bf16[256,1152]{1,0:T(8,128)(2,1)S(1)} %bitcast.17, bf16[256,1152]{1,0:T(8,128)(2,1)S(1)} %bitcast.20, bf16[256,1152]{1,0:T(8,128)(2,1)S(1)} %collective-permute-done.9.t1, bf16[256,1152]{1,0:T(8,128)(2,1)S(1)} %get-tuple-element.9.t2), custom_call_target="tpu_custom_call" | custom-call | bytes 2097152 | tf_op jit(solution)/shard_map/pallas_call | solution.py:186
  85.4 13.1 %collective-permute-done.10.code = bf16[272,1152]{1,0:T(8,128)(2,1)S(1)} collective-permute-done((bf16[272,1152]{1,0:T(8,128)(2,1)S(1)}, bf16[272,1152]{1,0:T(8,128)(2,1)S(1)}, u32[]{:S(2)}, u32[]{:S(2)}) %collective-permute-start.10) | collective-permute-done | bytes 626720 | tf_op jit(solution)/shard_map/ppermute | solution.py:184
  98.5 2.0 %shard_map.48 = f32[256,1152]{1,0:T(8,128)} custom-call(bf16[272,1152]{1,0:T(8,128)(2,1)S(1)} %collective-permute-done.10.code), custom_call_target="tpu_custom_call" | custom-call | bytes 2097152 | tf_op jit(solution)/shard_map/pallas_call | solution.py:188
  (13 shorter events, 0.1 us)
Async XLA Ops:
  0.6 21.4 %copy-start = (bf16[1,1,256,1152]{3,2,1,0:T(8,128)(2,1)S(1)}, bf16[1,1,256,1152]{3,2,1,0:T(8,128)(2,1)}, u32[]{:S(2)}) copy-start(bf16[1,1,256,1152]{3,2,1,0:T(8,128)(2,1)} %param.2) | copy-start | bytes 1769476
  0.6 5.8 %copy-start.1 = (bf16[1,1,256,1152]{3,2,1,0:T(8,128)(2,1)S(1)}, bf16[1,1,256,1152]{3,2,1,0:T(8,128)(2,1)}, u32[]{:S(2)}) copy-start(bf16[1,1,256,1152]{3,2,1,0:T(8,128)(2,1)} %param.3) | copy-start | bytes 1769476
  1.8 16.1 %collective-permute-start.6 = (bf16[128,1152]{1,0:T(8,128)(2,1)S(1)}, bf16[128,1152]{1,0:T(8,128)(2,1)}, u32[]{:S(2)}, u32[]{:S(2)}) collective-permute-start(bf16[128,1152]{1,0:T(8,128)(2,1)S(1)} %get-tuple-element.10), channel_id=1, source_target_pairs={{192,64},{224,32},{193,65},{225,33},{194,66},{226,34},{195,67},{22... | collective-permute-start | bytes 884744 | tf_op jit(solution)/shard_map/ppermute | solution.py:40
  3.9 15.5 %collective-permute-start.4 = (bf16[128,1152]{1,0:T(8,128)(2,1)S(1)}, bf16[128,1152]{1,0:T(8,128)(2,1)}, u32[]{:S(2)}, u32[]{:S(2)}) collective-permute-start(bf16[128,1152]{1,0:T(8,128)(2,1)S(1)} %get-tuple-element.11), channel_id=1, source_target_pairs={{192,0},{224,160},{193,1},{225,161},{194,2},{226,162},{195,3},{227... | collective-permute-start | bytes 884744 | tf_op jit(solution)/shard_map/ppermute | solution.py:40
  7.2 13.5 %collective-permute-start = (bf16[128,1152]{1,0:T(8,128)(2,1)S(1)}, bf16[128,1152]{1,0:T(8,128)(2,1)}, u32[]{:S(2)}, u32[]{:S(2)}) collective-permute-start(bf16[128,1152]{1,0:T(8,128)(2,1)S(1)} %get-tuple-element.13), channel_id=1, source_target_pairs={{192,128},{224,96},{193,129},{225,97},{194,130},{226,98},{195,131}... | collective-permute-start | bytes 884744 | tf_op jit(solution)/shard_map/ppermute | solution.py:40
  9.2 14.6 %collective-permute-start.2 = (bf16[128,1152]{1,0:T(8,128)(2,1)}, bf16[128,1152]{1,0:T(8,128)(2,1)}, u32[]{:S(2)}, u32[]{:S(2)}) collective-permute-start(bf16[128,1152]{1,0:T(8,128)(2,1)} %get-tuple-element.12), channel_id=1, source_target_pairs={{192,256},{224,288},{193,257},{225,289},{194,258},{226,290},{195,2... | collective-permute-start | bytes 884744 | tf_op jit(solution)/shard_map/ppermute | solution.py:40
  17.9 5.8 %collective-permute-start.7 = (bf16[128,1152]{1,0:T(8,128)(2,1)}, bf16[128,1152]{1,0:T(8,128)(2,1)}, u32[]{:S(2)}, u32[]{:S(2)}) collective-permute-start(bf16[128,1152]{1,0:T(8,128)(2,1)} %collective-permute-done.6), channel_id=1, source_target_pairs={{64,256},{32,288},{65,257},{33,289},{66,258},{34,290},{67,259},{35... | collective-permute-start | bytes 884744 | tf_op jit(solution)/shard_map/ppermute | solution.py:40
  19.3 4.4 %collective-permute-start.5 = (bf16[128,1152]{1,0:T(8,128)(2,1)}, bf16[128,1152]{1,0:T(8,128)(2,1)}, u32[]{:S(2)}, u32[]{:S(2)}) collective-permute-start(bf16[128,1152]{1,0:T(8,128)(2,1)} %collective-permute-done.4), channel_id=1, source_target_pairs={{0,256},{160,288},{1,257},{161,289},{2,258},{162,290},{3,259},{163... | collective-permute-start | bytes 884744 | tf_op jit(solution)/shard_map/ppermute | solution.py:40
  20.7 3.1 %collective-permute-start.1 = (bf16[128,1152]{1,0:T(8,128)(2,1)}, bf16[128,1152]{1,0:T(8,128)(2,1)}, u32[]{:S(2)}, u32[]{:S(2)}) collective-permute-start(bf16[128,1152]{1,0:T(8,128)(2,1)} %collective-permute-done), channel_id=1, source_target_pairs={{128,256},{96,288},{129,257},{97,289},{130,258},{98,290},{131,259}... | collective-permute-start | bytes 884744 | tf_op jit(solution)/shard_map/ppermute | solution.py:40
  22.3 40.2 %collective-permute-start.3 = (bf16[512,1152]{1,0:T(8,128)(2,1)S(1)}, bf16[512,1152]{1,0:T(8,128)(2,1)S(1)}, u32[]{:S(2)}, u32[]{:S(2)}) collective-permute-start(bf16[512,1152]{1,0:T(8,128)(2,1)S(1)} %shard_map.41), channel_id=1, source_target_pairs={{0,64},{32,96},{64,128},{96,160},{128,192},{160,224},{1,65},{33,97... | collective-permute-start | bytes 3538952 | tf_op jit(solution)/shard_map/ppermute | solution.py:40
  63.2 8.3 %collective-permute-start.8 = (bf16[256,1152]{1,0:T(8,128)(2,1)S(1)}, bf16[256,1152]{1,0:T(8,128)(2,1)S(1)}, u32[]{:S(2)}, u32[]{:S(2)}) collective-permute-start(bf16[256,1152]{1,0:T(8,128)(2,1)S(1)} %get-tuple-element.8), channel_id=1, source_target_pairs={{0,32},{32,0},{64,96},{96,64},{128,160},{160,128},{192,224},{224,1... | collective-permute-start | bytes 1769480 | tf_op jit(solution)/shard_map/ppermute | solution.py:40
  73.2 25.3 %collective-permute-start.10 = (bf16[272,1152]{1,0:T(8,128)(2,1)S(1)}, bf16[272,1152]{1,0:T(8,128)(2,1)S(1)}, u32[]{:S(2)}, u32[]{:S(2)}) collective-permute-start(bf16[272,1152]{1,0:T(8,128)(2,1)S(1)} %shard_map.45.code), channel_id=1, source_target_pairs={{0,1},{1,2},{2,3},{3,4},{4,5},{5,6},{6,7},{7,8},{8,9},{9,10},{10,1... | collective-permute-start | bytes 1880072 | tf_op jit(solution)/shard_map/ppermute | solution.py:184
  78.7 3.9 %collective-permute-start.9 = (bf16[256,1152]{1,0:T(8,128)(2,1)S(1)}, bf16[256,1152]{1,0:T(8,128)(2,1)S(1)}, u32[]{:S(2)}, u32[]{:S(2)}) collective-permute-start(bf16[256,1152]{1,0:T(8,128)(2,1)S(1)} %shard_map.46), channel_id=1, source_target_pairs={{0,32},{32,0},{64,96},{96,64},{128,160},{160,128},{192,224},{224,1... | collective-permute-start | bytes 1769480 | tf_op jit(solution)/shard_map/ppermute | solution.py:40

commit v6 on v4

--- a/solution.py
+++ b/solution.py
@@ -74,26 +74,32 @@
 
 
 def after_kernel(own, after, sent):
-    sent[...] = own[sent.shape[0] :]
-
-
-def pick_images(where, out0, far0, out1, far1, i0, i2, swap):
+    sent[...] = own[own.shape[0] - sent.shape[0] :]
+
+
+def swap_images(where, out0, far0, out1, far1, i0, swap):
     half = far0.shape[0]
+
+    @pl.when(where[0] == 1)
+    def _():
+        choose(where[1], out0, far0, swap.at[:half])
+        choose(where[2], out1, far1, swap.at[half:])
+
+    @pl.when(where[0] == 0)
+    def _():
+        swap[...] = i0[...]
+
+
+def all_kernel(far2, straight, swap, done):
+    done[...] = jnp.zeros_like(done)
+
+
+def part_kernel(where, done, out0, far0, out1, far1, out2, far2, straight, near, i0, t2, out, i2):
+    half, cut = far0.shape[0], far2.shape[0]
     choose(where[1], out0, far0, i2.at[:half])
     choose(where[2], out1, far1, i2.at[half:])
-    choose(where[0], i2, i0, swap)
-
-
-def pick_texts(where, out2, far2, straight, picked):
-    half = far2.shape[0]
-    choose(where[3], out2, far2, picked.at[:half])
-    picked[half:] = straight[...]
-
-
-def part_kernel(where, picked, near, i2, i0, t2, out):
-    half = near.shape[0]
-    t2[:half] = picked[:half]
-    choose(where[4], picked.at[half:], near, t2.at[half:])
+    choose(where[3], out2, far2, t2.at[:cut])
+    choose(where[4], straight, near, t2.at[cut:])
     text = t2[...]
     out[...] = dot_tn(coefs(i2[...], text, True), i2[...]) + dot_tn(coefs(i0[...], text, False), i0[...])
 
@@ -169,26 +175,29 @@
 
     full = jax.ShapeDtypeStruct((rows, width), jnp.float32)
 
-    pieces = (own_i[:half], own_i[half:], own_t[:half])
+    cut = rows // 2
+    pieces = (own_i[:half], own_i[half:], own_t[:cut])
     out = [move(p, t) for p, t in zip(pieces, MOVE_OUT)]
-    straight = move(own_t[half:], MOVE_STRAIGHT)
+    straight = move(own_t[cut:], MOVE_STRAIGHT)
     far = []
     for q, o, p, t in zip(plane, out, pieces, MOVE_ON):
         relay = (x == q).astype(jnp.int32).reshape(1)
-        far.append(move(call(relay_kernel, bf(half), [sm] + [vm] * 2, 0)(relay, o, p), t))
-    near = move(call(after_kernel, bf(half), [vm, anywhere], 0)(own_t, out[2]), MOVE_NEAR)
-    i2, swap_i = call(pick_images, (bf(rows),) * 2, [sm] + [vm] * 5, 0)(where, out[0], far[0], out[1], far[1], own_i)
-    i1 = move(swap_i, MOVE_SWAP)
-    picked = call(pick_texts, bf(rows), [sm] + [vm] * 3, 20)(where, out[2], far[2], straight)
-    t2, part = call(part_kernel, (bf(rows), full), [sm] + [vm] * 4, 60)(where, picked, near, i2, own_i)
+        far.append(move(call(relay_kernel, bf(p.shape[0]), [sm] + [vm] * 2, 0)(relay, o, p), t))
+    near = move(call(after_kernel, bf(rows - cut), [vm, anywhere], 0)(own_t, out[2]), MOVE_NEAR)
+    swap = call(swap_images, bf(rows), [sm] + [vm] * 5, 0)(where, out[0], far[0], out[1], far[1], own_i)
+    i1 = move(swap, MOVE_SWAP)
+    done = call(all_kernel, jax.ShapeDtypeStruct((8, 128), jnp.float32), [anywhere] * 3, 20)(far[2], straight, swap)
+    t2, part = call(
+        part_kernel, (bf(rows), full), [sm, anywhere] + [vm] * 9, 60, scratch=[pltpu.VMEM((rows, width), jnp.bfloat16)]
+    )(where, done, out[0], far[0], out[1], far[1], out[2], far[2], straight, near, own_i)
     code = call(text_kernel, bf(rows + EXTRA), [vm] * 3, 1)(part, i1, t2)
     count = lax.axis_size("group")
     got = lax.ppermute(code, "group", [(s, (s + 1) % count) for s in range(count)])
     t1 = move(call(swap_texts, bf(rows), [sm, anywhere] + [vm] * 2, 0)(where, code, t2, own_t), MOVE_SWAP)
     image_grad = call(image_kernel, full, [vm] * 4, 0)(own_i, own_t, t1, t2)
-    cut = rows // 4
+    step = rows // 4
     text_grad = call(
-        read_kernel, full, [vm], 0, out_specs=pl.BlockSpec((cut, width), lambda n: (n, 0)), grid=(rows // cut,)
+        read_kernel, full, [vm], 0, out_specs=pl.BlockSpec((step, width), lambda n: (n, 0)), grid=(rows // step,)
     )(got)
     return image_grad.reshape(images.shape), text_grad.reshape(texts.shape)
 

time: 93.9 us -> 90.6 us (0.965)
  starting transfers between devices: 65.9 us -> 61.7 us
  waiting for transfers between devices: 13.4 us -> 14.6 us
    ppermute x10, starting transfers between devices: 62.8 us -> 58.5 us  [move(): return lax.ppermute(value, AXES, table)]
    ppermute x10, waiting for transfers between devices: 6.66 us -> 7.95 us  [move(): return lax.ppermute(value, AXES, table)]
where the time goes in v6:
time: 90.6 us; the launch traced here: 89.9 us
  starting transfers between devices  61.7 us (68%)
  waiting for transfers between devices  14.6 us (16%)
  Pallas kernels  10.7 us (12%)
  local copies, waits for them, and re-layouts  2.02 us (2%)
  between operations  0.91 us (1%)
    ppermute x10, starting transfers between devices, move(): return lax.ppermute(value, AXES, table)  58.5 us
    ppermute x10, waiting for transfers between devices, move(): return lax.ppermute(value, AXES, table)  7.95 us
    ppermute x1, waiting for transfers between devices, body(): lax.ppermute(code, 'group', [(s, (s + 1) % count) for s in range(count)])  6.63 us
    ppermute x1, starting transfers between devices, body(): lax.ppermute(code, 'group', [(s, (s + 1) % count) for s in range(count)])  3.16 us
    pallas_call x1, Pallas kernels, body(): image_grad = call(image_kernel, full, [vm] * 4, 0)(own_i, own_t, t1, t2)  2.76 us
    pallas_call x1, Pallas kernels, body(): call(part_kernel, (bf(rows), full), [sm, anywhere] + [vm] * 9, 60, scratc...  2.25 us
    pallas_call x1, Pallas kernels, body(): call(read_kernel, full, [vm], 0, out_specs=pl.BlockSpec((step, width), la...  2.03 us
  transfers between devices with their start and end apart: 11, of which 5 were waited for; matrix products, arithmetic and copies ran while one was open for 1% of the time, Pallas kernels for 8%

profile of v6, /device:TPU:1, one launch (start us, length us, event | category | flops | bytes accessed | tf_op | source)
XLA Modules:
  0.0 89.9 jit_solution(14434889320455390902)
XLA Ops:
  0.6 1.2 %slice_bitcast_fusion = (bf16[128,1152]{1,0:T(8,128)(2,1)S(1)}, bf16[128,1152]{1,0:T(8,128)(2,1)S(1)}) fusion(bf16[1,1,256,1152]{3,2,1,0:T(8,128)(2,1)} %param.2), kind=kLoop, calls=%fused_computation | loop fusion | bytes 1179648 | tf_op jit(solution)/shard_map/slice | solution.py:179
  1.8 3.9 %collective-permute-start.5 = (bf16[128,1152]{1,0:T(8,128)(2,1)S(1)}, bf16[128,1152]{1,0:T(8,128)(2,1)S(1)}, u32[]{:S(2)}, u32[]{:S(2)}) collective-permute-start(bf16[128,1152]{1,0:T(8,128)(2,1)S(1)} %get-tuple-element.6.own), channel_id=1, source_target_pairs={{192,64},{64,128},{224,32},{32,96},{193,65},{65,129},{225,33},{33,... | collective-permute-start | bytes 884744 | tf_op jit(solution)/shard_map/ppermute | solution.py:42
  5.8 0.7 collective-permute-start.3
  6.5 0.8 slice_bitcast_fusion.2
  7.2 0.7 collective-permute-start
  7.9 1.3 %collective-permute-start.2 = (bf16[128,1152]{1,0:T(8,128)(2,1)}, bf16[128,1152]{1,0:T(8,128)(2,1)}, u32[]{:S(2)}, u32[]{:S(2)}) collective-permute-start(bf16[128,1152]{1,0:T(8,128)(2,1)} %get-tuple-element.8), channel_id=1, source_target_pairs={{192,256},{224,288},{193,257},{225,289},{194,258},{226,290},{195,2... | collective-permute-start | bytes 884744 | tf_op jit(solution)/shard_map/ppermute | solution.py:42
  9.2 1.3 %collective-permute-done.5.out.out1 = bf16[128,1152]{1,0:T(8,128)(2,1)S(1)} collective-permute-done((bf16[128,1152]{1,0:T(8,128)(2,1)S(1)}, bf16[128,1152]{1,0:T(8,128)(2,1)S(1)}, u32[]{:S(2)}, u32[]{:S(2)}) %collective-permute-start.5) | collective-permute-done | bytes 294944 | tf_op jit(solution)/shard_map/ppermute | solution.py:42
  10.5 11.4 %collective-permute-start.6 = (bf16[128,1152]{1,0:T(8,128)(2,1)S(1)}, bf16[128,1152]{1,0:T(8,128)(2,1)S(1)}, u32[]{:S(2)}, u32[]{:S(2)}) collective-permute-start(bf16[128,1152]{1,0:T(8,128)(2,1)S(1)} %shard_map.43), channel_id=1, source_target_pairs={{0,64},{32,288},{64,256},{96,160},{128,192},{160,224},{1,65},{33,2... | collective-permute-start | bytes 884744 | tf_op jit(solution)/shard_map/ppermute | solution.py:42
  22.0 0.7 shard_map.42
  22.7 2.0 %collective-permute-start.4 = (bf16[128,1152]{1,0:T(8,128)(2,1)}, bf16[128,1152]{1,0:T(8,128)(2,1)S(1)}, u32[]{:S(2)}, u32[]{:S(2)}) collective-permute-start(bf16[128,1152]{1,0:T(8,128)(2,1)} %shard_map.42), channel_id=1, source_target_pairs={{0,256},{32,96},{64,128},{96,160},{128,192},{160,288},{1,257},{33,... | collective-permute-start | bytes 884744 | tf_op jit(solution)/shard_map/ppermute | solution.py:42
  24.8 4.3 %collective-permute-start.1 = (bf16[128,1152]{1,0:T(8,128)(2,1)S(1)}, bf16[128,1152]{1,0:T(8,128)(2,1)}, u32[]{:S(2)}, u32[]{:S(2)}) collective-permute-start(bf16[128,1152]{1,0:T(8,128)(2,1)S(1)} %shard_map.41), channel_id=1, source_target_pairs={{0,64},{32,96},{64,128},{96,288},{128,256},{160,224},{1,65},{33,97... | collective-permute-start | bytes 884744 | tf_op jit(solution)/shard_map/ppermute | solution.py:42
  29.3 9.4 %collective-permute-start.7 = (bf16[128,1152]{1,0:T(8,128)(2,1)S(1)}, bf16[128,1152]{1,0:T(8,128)(2,1)S(1)}, u32[]{:S(2)}, u32[]{:S(2)}) collective-permute-start(bf16[128,1152]{1,0:T(8,128)(2,1)S(1)} %shard_map.46), channel_id=1, source_target_pairs={{0,64},{32,96},{64,128},{96,160},{128,192},{160,224},{1,65},{33,97... | collective-permute-start | bytes 884744 | tf_op jit(solution)/shard_map/ppermute | solution.py:42
  38.7 1.9 %collective-permute-done.4.far0 = bf16[128,1152]{1,0:T(8,128)(2,1)S(1)} collective-permute-done((bf16[128,1152]{1,0:T(8,128)(2,1)}, bf16[128,1152]{1,0:T(8,128)(2,1)S(1)}, u32[]{:S(2)}, u32[]{:S(2)}) %collective-permute-start.4) | collective-permute-done | bytes 294944 | tf_op jit(solution)/shard_map/ppermute | solution.py:42
  40.7 0.6 shard_map.44.swap
  41.3 17.6 %collective-permute-start.8 = (bf16[256,1152]{1,0:T(8,128)(2,1)S(1)}, bf16[256,1152]{1,0:T(8,128)(2,1)S(1)}, u32[]{:S(2)}, u32[]{:S(2)}) collective-permute-start(bf16[256,1152]{1,0:T(8,128)(2,1)S(1)} %shard_map.44.swap), channel_id=1, source_target_pairs={{0,32},{32,0},{64,96},{96,64},{128,160},{160,128},{192,224},{224,1... | collective-permute-start | bytes 1769480 | tf_op jit(solution)/shard_map/ppermute | solution.py:42
  58.9 3.1 %collective-permute-done.1.far2 = bf16[128,1152]{1,0:T(8,128)(2,1)} collective-permute-done((bf16[128,1152]{1,0:T(8,128)(2,1)S(1)}, bf16[128,1152]{1,0:T(8,128)(2,1)}, u32[]{:S(2)}, u32[]{:S(2)}) %collective-permute-start.1) | collective-permute-done | bytes 294944 | tf_op jit(solution)/shard_map/ppermute | solution.py:42
  62.0 2.2 %shard_map.47 = (bf16[256,1152]{1,0:T(8,128)(2,1)S(1)}, f32[256,1152]{1,0:T(8,128)S(1)}) custom-call(s32[5]{0:T(128)S(1)} %stack.39.where, f32[8,128]{1,0:T(8,128)S(1)} %shard_map.45.done, bf16[128,1152]{1,0:T(8,128)(2,1)S(1)} %collective-permute-done.3.out.out0, bf16[128,1152]{1,0:T(8,128)(2,1)S(1)} %collective-permute-done.4.far0, ...), custom_call_target="tpu_custom_call" | custom-call | flops 18119393280 | bytes 2097152 | tf_op jit(solution)/shard_map/pallas_call | solution.py:190
  64.3 1.7 %shard_map.48.code = bf16[272,1152]{1,0:T(8,128)(2,1)S(1)} custom-call(f32[256,1152]{1,0:T(8,128)S(1)} %get-tuple-element.4.part, bf16[256,1152]{1,0:T(8,128)(2,1)S(1)} %collective-permute-done.8.i1, bf16[256,1152]{1,0:T(8,128)(2,1)S(1)} %get-tuple-element.5.t2), custom_call_target="tpu_custom_call" | custom-call | flops 301989888 | bytes 2097152 | tf_op jit(solution)/shard_map/pallas_call | solution.py:193
  66.0 3.2 %collective-permute-start.10 = (bf16[272,1152]{1,0:T(8,128)(2,1)S(1)}, bf16[272,1152]{1,0:T(8,128)(2,1)S(1)}, u32[]{:S(2)}, u32[]{:S(2)}) collective-permute-start(bf16[272,1152]{1,0:T(8,128)(2,1)S(1)} %shard_map.48.code), channel_id=1, source_target_pairs={{0,1},{1,2},{2,3},{3,4},{4,5},{5,6},{6,7},{7,8},{8,9},{9,10},{10,1... | collective-permute-start | bytes 1880072 | tf_op jit(solution)/shard_map/ppermute | solution.py:195
  69.7 7.1 %collective-permute-start.9 = (bf16[256,1152]{1,0:T(8,128)(2,1)S(1)}, bf16[256,1152]{1,0:T(8,128)(2,1)S(1)}, u32[]{:S(2)}, u32[]{:S(2)}) collective-permute-start(bf16[256,1152]{1,0:T(8,128)(2,1)S(1)} %shard_map.49), channel_id=1, source_target_pairs={{0,32},{32,0},{64,96},{96,64},{128,160},{160,128},{192,224},{224,1... | collective-permute-start | bytes 1769480 | tf_op jit(solution)/shard_map/ppermute | solution.py:42
  76.9 1.6 %collective-permute-done.9.t1 = bf16[256,1152]{1,0:T(8,128)(2,1)S(1)} collective-permute-done((bf16[256,1152]{1,0:T(8,128)(2,1)S(1)}, bf16[256,1152]{1,0:T(8,128)(2,1)S(1)}, u32[]{:S(2)}, u32[]{:S(2)}) %collective-permute-start.9) | collective-permute-done | bytes 589856 | tf_op jit(solution)/shard_map/ppermute | solution.py:42
  78.5 2.8 %shard_map.50 = f32[256,1152]{1,0:T(8,128)} custom-call(bf16[256,1152]{1,0:T(8,128)(2,1)S(1)} %bitcast.25, bf16[256,1152]{1,0:T(8,128)(2,1)S(1)} %bitcast.22, bf16[256,1152]{1,0:T(8,128)(2,1)S(1)} %collective-permute-done.9.t1, bf16[256,1152]{1,0:T(8,128)(2,1)S(1)} %get-tuple-element.5.t2), custom_call_target="tpu_custom_call" | custom-call | bytes 2097152 | tf_op jit(solution)/shard_map/pallas_call | solution.py:197
  81.2 6.6 %collective-permute-done.10.code = bf16[272,1152]{1,0:T(8,128)(2,1)S(1)} collective-permute-done((bf16[272,1152]{1,0:T(8,128)(2,1)S(1)}, bf16[272,1152]{1,0:T(8,128)(2,1)S(1)}, u32[]{:S(2)}, u32[]{:S(2)}) %collective-permute-start.10) | collective-permute-done | bytes 626720 | tf_op jit(solution)/shard_map/ppermute | solution.py:195
  87.9 2.0 %shard_map.51 = f32[256,1152]{1,0:T(8,128)} custom-call(bf16[272,1152]{1,0:T(8,128)(2,1)S(1)} %collective-permute-done.10.code), custom_call_target="tpu_custom_call" | custom-call | bytes 2097152 | tf_op jit(solution)/shard_map/pallas_call | solution.py:199
  (16 shorter events, 0.8 us)
Async XLA Ops:
  0.6 5.8 %copy-start = (bf16[1,1,256,1152]{3,2,1,0:T(8,128)(2,1)S(1)}, bf16[1,1,256,1152]{3,2,1,0:T(8,128)(2,1)}, u32[]{:S(2)}) copy-start(bf16[1,1,256,1152]{3,2,1,0:T(8,128)(2,1)} %param.3) | copy-start | bytes 1769476
  1.8 8.7 %collective-permute-start.5 = (bf16[128,1152]{1,0:T(8,128)(2,1)S(1)}, bf16[128,1152]{1,0:T(8,128)(2,1)S(1)}, u32[]{:S(2)}, u32[]{:S(2)}) collective-permute-start(bf16[128,1152]{1,0:T(8,128)(2,1)S(1)} %get-tuple-element.6.own), channel_id=1, source_target_pairs={{192,64},{64,128},{224,32},{32,96},{193,65},{65,129},{225,33},{33,... | collective-permute-start | bytes 884744 | tf_op jit(solution)/shard_map/ppermute | solution.py:42
  5.8 16.2 %collective-permute-start.3 = (bf16[128,1152]{1,0:T(8,128)(2,1)S(1)}, bf16[128,1152]{1,0:T(8,128)(2,1)S(1)}, u32[]{:S(2)}, u32[]{:S(2)}) collective-permute-start(bf16[128,1152]{1,0:T(8,128)(2,1)S(1)} %get-tuple-element.7.own), channel_id=1, source_target_pairs={{192,0},{0,64},{224,160},{160,224},{193,1},{1,65},{225,161},{161,2... | collective-permute-start | bytes 884744 | tf_op jit(solution)/shard_map/ppermute | solution.py:42
  7.2 17.6 %collective-permute-start = (bf16[128,1152]{1,0:T(8,128)(2,1)S(1)}, bf16[128,1152]{1,0:T(8,128)(2,1)S(1)}, u32[]{:S(2)}, u32[]{:S(2)}) collective-permute-start(bf16[128,1152]{1,0:T(8,128)(2,1)S(1)} %get-tuple-element.9.own), channel_id=1, source_target_pairs={{192,128},{128,192},{224,96},{96,160},{193,129},{129,193},{225,97}... | collective-permute-start | bytes 884744 | tf_op jit(solution)/shard_map/ppermute | solution.py:42
  7.9 51.0 %collective-permute-start.2 = (bf16[128,1152]{1,0:T(8,128)(2,1)}, bf16[128,1152]{1,0:T(8,128)(2,1)}, u32[]{:S(2)}, u32[]{:S(2)}) collective-permute-start(bf16[128,1152]{1,0:T(8,128)(2,1)} %get-tuple-element.8), channel_id=1, source_target_pairs={{192,256},{224,288},{193,257},{225,289},{194,258},{226,290},{195,2... | collective-permute-start | bytes 884744 | tf_op jit(solution)/shard_map/ppermute | solution.py:42
  10.5 28.2 %collective-permute-start.6 = (bf16[128,1152]{1,0:T(8,128)(2,1)S(1)}, bf16[128,1152]{1,0:T(8,128)(2,1)S(1)}, u32[]{:S(2)}, u32[]{:S(2)}) collective-permute-start(bf16[128,1152]{1,0:T(8,128)(2,1)S(1)} %shard_map.43), channel_id=1, source_target_pairs={{0,64},{32,288},{64,256},{96,160},{128,192},{160,224},{1,65},{33,2... | collective-permute-start | bytes 884744 | tf_op jit(solution)/shard_map/ppermute | solution.py:42
  22.7 17.9 %copy-start.1 = (bf16[1,1,256,1152]{3,2,1,0:T(8,128)(2,1)S(1)}, bf16[1,1,256,1152]{3,2,1,0:T(8,128)(2,1)}, u32[]{:S(2)}) copy-start(bf16[1,1,256,1152]{3,2,1,0:T(8,128)(2,1)} %param.2) | copy-start | bytes 1769476
  22.7 17.9 %collective-permute-start.4 = (bf16[128,1152]{1,0:T(8,128)(2,1)}, bf16[128,1152]{1,0:T(8,128)(2,1)S(1)}, u32[]{:S(2)}, u32[]{:S(2)}) collective-permute-start(bf16[128,1152]{1,0:T(8,128)(2,1)} %shard_map.42), channel_id=1, source_target_pairs={{0,256},{32,96},{64,128},{96,160},{128,192},{160,288},{1,257},{33,... | collective-permute-start | bytes 884744 | tf_op jit(solution)/shard_map/ppermute | solution.py:42
  24.8 37.2 %collective-permute-start.1 = (bf16[128,1152]{1,0:T(8,128)(2,1)S(1)}, bf16[128,1152]{1,0:T(8,128)(2,1)}, u32[]{:S(2)}, u32[]{:S(2)}) collective-permute-start(bf16[128,1152]{1,0:T(8,128)(2,1)S(1)} %shard_map.41), channel_id=1, source_target_pairs={{0,64},{32,96},{64,128},{96,288},{128,256},{160,224},{1,65},{33,97... | collective-permute-start | bytes 884744 | tf_op jit(solution)/shard_map/ppermute | solution.py:42
  29.3 32.7 %collective-permute-start.7 = (bf16[128,1152]{1,0:T(8,128)(2,1)S(1)}, bf16[128,1152]{1,0:T(8,128)(2,1)S(1)}, u32[]{:S(2)}, u32[]{:S(2)}) collective-permute-start(bf16[128,1152]{1,0:T(8,128)(2,1)S(1)} %shard_map.46), channel_id=1, source_target_pairs={{0,64},{32,96},{64,128},{96,160},{128,192},{160,224},{1,65},{33,97... | collective-permute-start | bytes 884744 | tf_op jit(solution)/shard_map/ppermute | solution.py:42
  41.3 23.0 %collective-permute-start.8 = (bf16[256,1152]{1,0:T(8,128)(2,1)S(1)}, bf16[256,1152]{1,0:T(8,128)(2,1)S(1)}, u32[]{:S(2)}, u32[]{:S(2)}) collective-permute-start(bf16[256,1152]{1,0:T(8,128)(2,1)S(1)} %shard_map.44.swap), channel_id=1, source_target_pairs={{0,32},{32,0},{64,96},{96,64},{128,160},{160,128},{192,224},{224,1... | collective-permute-start | bytes 1769480 | tf_op jit(solution)/shard_map/ppermute | solution.py:42
  66.0 21.9 %collective-permute-start.10 = (bf16[272,1152]{1,0:T(8,128)(2,1)S(1)}, bf16[272,1152]{1,0:T(8,128)(2,1)S(1)}, u32[]{:S(2)}, u32[]{:S(2)}) collective-permute-start(bf16[272,1152]{1,0:T(8,128)(2,1)S(1)} %shard_map.48.code), channel_id=1, source_target_pairs={{0,1},{1,2},{2,3},{3,4},{4,5},{5,6},{6,7},{7,8},{8,9},{9,10},{10,1... | collective-permute-start | bytes 1880072 | tf_op jit(solution)/shard_map/ppermute | solution.py:195
  69.7 8.7 %collective-permute-start.9 = (bf16[256,1152]{1,0:T(8,128)(2,1)S(1)}, bf16[256,1152]{1,0:T(8,128)(2,1)S(1)}, u32[]{:S(2)}, u32[]{:S(2)}) collective-permute-start(bf16[256,1152]{1,0:T(8,128)(2,1)S(1)} %shard_map.49), channel_id=1, source_target_pairs={{0,32},{32,0},{64,96},{96,64},{128,160},{160,128},{192,224},{224,1... | collective-permute-start | bytes 1769480 | tf_op jit(solution)/shard_map/ppermute | solution.py:42
